TPU v7x, 256 devices: a whole 4x4x8 slice. The times are simulated.
256 devices in a mesh: row: 8 (over x_lo, y), col: 32 (over z, x_hi, core).
Axes of the slice: x: 4 (x_hi: 2, x_lo: 2; x = x_hi * 2 + x_lo), y: 4, z: 8, core: 2. Of those that a mesh axis runs over, the one named last changes fastest.
Arguments:
- latent: bfloat16 [512, 1024, 320], P('row', 'col')
- stale_input: bfloat16 [512, 1024, 320], P('row', 'col')
- stale_hidden: bfloat16 [512, 1024, 320], P('row', 'col')
- refresh: int32 [64, 32], P('row', 'col'), may hold values from 0 to 1, as said below
- gain_one: float32 [320], replicated, may hold values from 0.1 to 1.9
- weight_one: bfloat16 [9, 320, 320], replicated, may hold values from -0.109375 to 0.109375
- time_shift: float32 [320], replicated, may hold values from -4 to 4
- gain_two: float32 [320], replicated, may hold values from 0.1 to 1.9
- weight_two: bfloat16 [9, 320, 320], replicated, may hold values from -0.109375 to 0.109375
Outputs:
- block_out: bfloat16 [512, 1024, 320], P('row', 'col')
- fresh_hidden: bfloat16 [512, 1024, 320], P('row', 'col')
Inputs may be any that keep to these rules, and one draw needn't show every extreme that they name: refresh[k, c] is 1 where strip k (rows k * 8 onward) of tile column c is recomputed. The tiles of tile columns c and c plus half the number of tile columns, in the same tile row, hold at most 8 such strips together. In every draw the tile of the first tile row in the middle tile column and the tile of the last tile row in the last tile column hold all 8, and their paired tiles none.
All inputs are finite; a program needn't handle non-finite values.
Results may differ from a plain program's by a relative error of at most 0.0035.
Values may be sent and summed in bfloat16 or wider, within the bound.
A program may use at most 128 MiB of HBM per device.

v0:
```python
import jax
import jax.numpy as jnp
from jax import lax
from jax.sharding import PartitionSpec as P

GROUPS = 32
SH = 8


EPSILON = 1e-05


def with_halo(cells, sides, width):
    for axis, dim in sides:
        count = lax.axis_size(axis)
        ends = count - 1
        head = lax.slice_in_dim(cells, 0, width, axis=dim)
        tail = lax.slice_in_dim(cells, cells.shape[dim] - width, cells.shape[dim], axis=dim)
        cells = jnp.concatenate(
            [
                lax.ppermute(tail, axis, [(i, (i + 1) % count) for i in range(ends)]),
                cells,
                lax.ppermute(head, axis, [((i + 1) % count, i) for i in range(ends)]),
            ],
            axis=dim,
        )
    return cells


def from_partner(value, axis, distance):
    mask = 2**distance
    pairs = [(source, source ^ mask) for source in range(lax.axis_size(axis))]
    return lax.ppermute(value, axis, pairs)


def group_sums(values):
    grouped = values.astype(jnp.float32).reshape(-1, GROUPS, values.shape[-1] // GROUPS)
    return jnp.stack([jnp.sum(grouped, axis=(0, 2)), jnp.sum(grouped * grouped, axis=(0, 2))])


def activate(values, center, spread, scaling):
    channels = values.shape[-1]
    grouped = values.astype(jnp.float32).reshape(values.shape[:-1] + (GROUPS, channels // GROUPS))
    scaled = ((grouped - center[:, None]) * spread[:, None]).reshape(values.shape)
    return jax.nn.silu(scaled * scaling).astype(jnp.bfloat16)


def convolve(window, weight):
    strip_total = window.shape[0]
    strip_rows = window.shape[1] - 2
    strip_cols = window.shape[2] - 2
    channels = window.shape[3]
    summed = jnp.zeros((strip_total * strip_rows * strip_cols, channels), jnp.float32)
    for tap_index in range(9):
        shift_row, shift_col = divmod(tap_index, 3)
        shifted = window[
            :, shift_row : shift_row + strip_rows, shift_col : shift_col + strip_cols
        ].reshape(-1, channels)
        summed = summed + jnp.dot(shifted, weight[tap_index], preferred_element_type=jnp.float32)
    return summed.reshape(strip_total, strip_rows, strip_cols, channels)


def refresh_strips(work, center, spread, gain_two, weight_one, weight_two, time_shift):
    hidden_new = (convolve(work[:, 0], weight_one) + time_shift).astype(jnp.bfloat16)
    second = activate(hidden_new, center[1], spread[1], gain_two)
    window_two = work[:, 1].at[:, 1:-1, 1:-1].set(second)
    finished = (
        work[:, 2, 1:-1, 1:-1].astype(jnp.float32) + convolve(window_two, weight_two)
    ).astype(jnp.bfloat16)
    return jnp.stack([finished, hidden_new], axis=1)


def per_device(
    latent,
    stale_input,
    stale_hidden,
    refresh,
    gain_one,
    weight_one,
    time_shift,
    gain_two,
    weight_two,
):
    tile_rows, tile_cols, channels = latent.shape
    strip_count = tile_rows // SH
    slot_count = strip_count // 2
    partial_sums = jnp.stack([group_sums(stale_input), group_sums(stale_hidden)])
    totals = lax.psum(partial_sums, ("row", "col"))
    cell_count = float(
        tile_rows * tile_cols * lax.axis_size("row") * lax.axis_size("col") * (channels // GROUPS)
    )
    center = totals[:, 0] / cell_count
    spread = lax.rsqrt(totals[:, 1] / cell_count - center * center + EPSILON)
    outgoing = jnp.stack(
        [
            activate(stale_input, center[0], spread[0], gain_one),
            activate(stale_hidden, center[1], spread[1], gain_two),
        ]
    )
    padded = with_halo(outgoing, (("row", 1), ("col", 2)), 1)
    current = activate(latent, center[0], spread[0], gain_one)
    first_windows = jnp.stack(
        [
            padded[0, strip_index * SH : strip_index * SH + SH + 2]
            for strip_index in range(strip_count)
        ]
    )
    second_windows = jnp.stack(
        [
            padded[1, strip_index * SH : strip_index * SH + SH + 2]
            for strip_index in range(strip_count)
        ]
    )
    first_windows = first_windows.at[:, 1:-1, 1:-1].set(
        current.reshape(strip_count, SH, tile_cols, channels)
    )
    latent_strips = latent.reshape(strip_count, SH, tile_cols, channels)
    latent_windows = jnp.pad(latent_strips, ((0, 0), (1, 1), (1, 1), (0, 0)))
    work = jnp.stack([first_windows, second_windows, latent_windows], axis=1)
    active = refresh[:, 0] > 0
    flags = active.astype(jnp.int32)
    ranking = jnp.cumsum(flags) - 1
    keep_count = jnp.minimum(jnp.sum(flags), slot_count)
    priority = jnp.where(active, ranking, strip_count + jnp.arange(strip_count, dtype=jnp.int32))
    ordering = jnp.argsort(priority)
    partner_bit = lax.axis_size("col").bit_length() - 2
    outgoing_strips = jnp.take(work, ordering[slot_count:], axis=0)
    incoming_strips = from_partner(outgoing_strips, "col", partner_bit)
    slot_ids = jnp.arange(slot_count, dtype=jnp.int32)
    candidates = jnp.concatenate([jnp.take(work, ordering[:slot_count], axis=0), incoming_strips])
    chosen_ids = jnp.where(slot_ids < keep_count, slot_ids, slot_count + slot_ids - keep_count)
    results = refresh_strips(
        jnp.take(candidates, chosen_ids, axis=0),
        center,
        spread,
        gain_two,
        weight_one,
        weight_two,
        time_shift,
    )
    returning = jnp.take(results, jnp.minimum(keep_count + slot_ids, slot_count - 1), axis=0)
    returned = from_partner(returning, "col", partner_bit)
    combined = jnp.concatenate([results, returned])
    finished = jnp.take(combined, jnp.clip(ranking, 0, strip_count - 1), axis=0)
    selector = active[:, None, None, None]
    block_out = jnp.where(selector, finished[:, 0], latent_strips).reshape(
        tile_rows, tile_cols, channels
    )
    old_hidden = stale_hidden.reshape(strip_count, SH, tile_cols, channels)
    fresh_hidden = jnp.where(selector, finished[:, 1], old_hidden).reshape(
        tile_rows, tile_cols, channels
    )
    return (block_out, fresh_hidden)


def solution(mesh):
    placed = (
        P("row", "col", None),
        P("row", "col", None),
        P("row", "col", None),
        P("row", "col"),
        P(),
        P(),
        P(),
        P(),
        P(),
    )
    return jax.shard_map(
        per_device,
        mesh=mesh,
        in_specs=placed,
        out_specs=(P("row", "col", None), P("row", "col", None)),
        check_vma=False,
    )
```

profile of v0, /device:TPU:125, one launch (start us, length us, event | category | flops | bytes accessed | tf_op | source)
XLA Modules:
  0.0 430.5 jit_solution(10771763924882072671)
XLA Ops:
  4.2 73.5 %psum.7 = f32[2,2,32]{2,1,0:T(2,128)S(1)} all-reduce(f32[2,2,32]{2,1,0:T(2,128)S(1)} %pad_maximum_fusion.11), channel_id=1, replica_groups=mesh['row'=8,'col'=32] {'row','col'}, use_global_device_ids=true, to_apply=%region_9.10 | all-reduce | flops 128 | bytes 1024 | tf_op jit(solution)/shard_map/psum | solution.py:88
  79.5 4.3 multiply_convert_fusion
  83.8 5.0 %collective-permute-start = (bf16[2,1,32,320]{3,2,1,0:T(8,128)(2,1)S(1)}, bf16[2,1,32,320]{3,2,1,0:T(8,128)(2,1)S(1)}, u32[]{:S(2)}, u32[]{:S(2)}) collective-permute-start(bf16[2,1,32,320]{3,2,1,0:T(8,128)(2,1)S(1)} %get-tuple-element.59), channel_id=1, source_target_pairs={{0,32},{32,64},{64,96},{96,128},{128,160},{160,192},{192,224},{1,3... | collective-permute-start | bytes 122888 | tf_op jit(solution)/shard_map/ppermute | solution.py:21
  90.8 2.4 pad_bitcast_fusion
  96.2 5.0 %collective-permute-start.2 = (bf16[2,66,1,320]{3,2,1,0:T(2,128)(2,1)S(1)}, bf16[2,66,1,320]{3,2,1,0:T(2,128)(2,1)S(1)}, u32[]{:S(2)}, u32[]{:S(2)}) collective-permute-start(bf16[2,66,1,320]{3,2,1,0:T(2,128)(2,1)S(1)} %get-tuple-element.55), channel_id=1, source_target_pairs={{0,1},{1,2},{2,3},{3,4},{4,5},{5,6},{6,7},{7,8},{8,9},{9,10},{10,1... | collective-permute-start | bytes 253448 | tf_op jit(solution)/shard_map/ppermute | solution.py:21
  103.9 8.0 %collective-permute-done.3 = bf16[2,66,1,320]{3,2,1,0:T(2,128)(2,1)S(1)} collective-permute-done((bf16[2,66,1,320]{3,2,1,0:T(2,128)(2,1)S(1)}, bf16[2,66,1,320]{3,2,1,0:T(2,128)(2,1)S(1)}, u32[]{:S(2)}, u32[]{:S(2)}) %collective-permute-start.3) | collective-permute-done | bytes 84512 | tf_op jit(solution)/shard_map/ppermute | solution.py:23
  111.9 4.3 %pad_maximum_fusion.2 = bf16[2,66,34,320]{3,2,1,0:T(8,128)(2,1)S(1)} fusion(bf16[2,66,1,320]{3,2,1,0:T(2,128)(2,1)S(1)} %collective-permute-done.3, bf16[2,1,32,320]{3,2,1,0:T(8,128)(2,1)S(1)} %collective-permute-done.1, bf16[1,64,32,320]{3,2,1,0:T(8,128)(2,1)S(1)} %fusion.18, bf16[1,64,32,320]{3,2,1,0:T(8,128)(2,1)S(1)} %get-tuple-element.79, ...), kind=kLoop, calls=%fused_computation.13 | loop fusion | flops 17233920 | bytes 5744640 | tf_op jit(solution)/shard_map/concatenate | solution.py:19
  120.1 19.2 %scatter.6 = bf16[8,1,10,34,320]{4,3,2,0,1:T(8,128)(2,1)} dynamic-update-slice(bf16[8,1,10,34,320]{4,3,2,0,1:T(8,128)(2,1)} %bitcast.167, bf16[8,1,8,32,320]{4,3,2,0,1:T(8,128)(2,1)} %bitcast.148, s32[]{:T(128)} %constant.110.clone.1, s32[]{:T(128)} %constant.110.clone.1, s32[]{:T(128)} %constant.118.clone.1, s32[]{:T(128)} %constant.118.clone.1, s32[]{:T(128)} %constant.110.clone.1) | dynamic-update-slice | bytes 2621444 | tf_op jit(solution)/shard_map/scatter | solution.py:114
  139.3 6.5 %pad_maximum_fusion = bf16[8,3,10,34,320]{4,3,2,1,0:T(8,128)(2,1)} fusion(bf16[8,1,10,34,320]{4,3,2,1,0:T(8,128)(2,1)S(1)} %copy-done.5, bf16[8,1,10,34,320]{4,3,2,1,0:T(8,128)(2,1)} %bitcast.169, bf16[8,1,10,34,320]{4,3,2,1,0:T(8,128)(2,1)} %bitcast.168), kind=kLoop, calls=%fused_computation.5 | loop fusion | flops 5222400 | bytes 10444800 | tf_op jit(solution)/shard_map/stack | solution.py:119
  145.8 6.1 %gather_fusion.3 = bf16[4,3,10,34,320]{4,3,2,1,0:T(8,128)(2,1)} fusion(bf16[8,3,10,34,320]{4,3,2,1,0:T(8,128)(2,1)} %pad_maximum_fusion, s32[1024]{0:T(1024)S(1)} %get-tuple-element.99), kind=kCustom, calls=%fused_computation.1.clone | custom fusion | bytes 5222416 | tf_op jit(solution)/shard_map/jit(_take)/gather | solution.py:127
  151.9 2.5 broadcast_select_fusion.1
  154.4 2.8 copy.29
  157.2 6.1 %gather_fusion.2 = bf16[4,3,10,34,320]{4,3,2,1,0:T(8,128)(2,1)} fusion(bf16[8,3,10,34,320]{4,3,2,1,0:T(8,128)(2,1)} %pad_maximum_fusion, s32[1024]{0:T(1024)S(1)} %get-tuple-element.97), kind=kCustom, calls=%fused_computation.clone | custom fusion | bytes 5222416 | tf_op jit(solution)/shard_map/jit(_take)/gather | solution.py:130
  163.3 2.5 broadcast_select_fusion.2
  165.8 130.6 %collective-permute-done.4 = bf16[4,3,10,34,320]{4,0,3,2,1:T(4,128)(2,1)} collective-permute-done((bf16[4,3,10,34,320]{4,0,3,2,1:T(4,128)(2,1)}, bf16[4,3,10,34,320]{4,0,3,2,1:T(4,128)(2,1)}, u32[]{:S(2)}, u32[]{:S(2)}) %collective-permute-start.4) | collective-permute-done | bytes 2611232 | tf_op jit(solution)/shard_map/ppermute | solution.py:33
  296.4 4.3 copy.30
  300.7 6.4 %pad_maximum_fusion.1 = bf16[8,3,10,34,320]{4,3,2,1,0:T(8,128)(2,1)} fusion(bf16[4,3,10,34,320]{4,3,2,1,0:T(8,128)(2,1)} %copy.30, bf16[4,3,10,34,320]{4,3,2,1,0:T(8,128)(2,1)S(1)} %broadcast_select_fusion.2), kind=kLoop, calls=%fused_computation.6 | loop fusion | flops 2611200 | bytes 10444800 | tf_op jit(solution)/shard_map/concatenate | solution.py:130
  307.1 6.1 %gather_fusion.4 = bf16[4,3,10,34,320]{4,3,2,1,0:T(8,128)(2,1)} fusion(bf16[8,3,10,34,320]{4,3,2,1,0:T(8,128)(2,1)} %pad_maximum_fusion.1, s32[1024]{0:T(1024)S(1)} %get-tuple-element.96), kind=kCustom, calls=%fused_computation.2.clone | custom fusion | bytes 5222416 | tf_op jit(solution)/shard_map/jit(_take)/gather | solution.py:133
  313.2 2.5 broadcast_select_fusion
  328.5 12.2 %scatter.9 = bf16[4,10,34,320]{3,2,1,0:T(8,128)(2,1)S(1)} dynamic-update-slice(bf16[4,10,34,320]{3,2,1,0:T(8,128)(2,1)S(1)} %get-tuple-element.53, bf16[4,8,32,320]{3,2,1,0:T(8,128)(2,1)} %multiply_convert_fusion.1, s32[]{:T(128)} %constant.110.clone.1, s32[]{:T(128)} %constant.118.clone.1, s32[]{:T(128)} %constant.118.clone.1, s32[]{:T(128)} %constant.110.clone.1) | dynamic-update-slice | bytes 1310724 | tf_op jit(solution)/shard_map/scatter | solution.py:66
  349.5 2.9 copy.32
  359.2 59.7 %collective-permute-done.5 = bf16[4,2,8,32,320]{4,3,2,1,0:T(8,128)(2,1)} collective-permute-done((bf16[4,2,8,32,320]{4,3,2,1,0:T(8,128)(2,1)S(1)}, bf16[4,2,8,32,320]{4,3,2,1,0:T(8,128)(2,1)}, u32[]{:S(2)}, u32[]{:S(2)}) %collective-permute-start.5) | collective-permute-done | bytes 1310752 | tf_op jit(solution)/shard_map/ppermute | solution.py:33
  418.9 2.4 pad_maximum_fusion.3
  421.3 2.6 gather_fusion.1
  (122 shorter events, 50.6 us)
Async XLA Ops:
  0.6 2.5 copy-start
  0.6 77.8 %copy-start.13 = (f32[320]{0:T(512)S(1)}, f32[320]{0:T(512)}, u32[]{:S(2)}) copy-start(f32[320]{0:T(512)} %param.22) | copy-start | bytes 3844
  3.1 76.3 %copy-start.15 = (f32[320]{0:T(512)S(1)}, f32[320]{0:T(512)}, u32[]{:S(2)}) copy-start(f32[320]{0:T(512)} %param.19) | copy-start | bytes 3844
  83.8 7.0 %copy-start.2 = (bf16[64,32,320]{2,1,0:T(8,128)(2,1)S(1)}, bf16[64,32,320]{2,1,0:T(8,128)(2,1)}, u32[]{:S(2)}) copy-start(bf16[64,32,320]{2,1,0:T(8,128)(2,1)} %param.15) | copy-start | bytes 3932164
  83.8 9.4 %copy-start.16 = (s32[8,1]{0,1:T(1,128)S(1)}, s32[8,1]{0,1:T(1,128)}, u32[]{:S(2)}) copy-start(s32[8,1]{0,1:T(1,128)} %param.18) | copy-start | bytes 100
  83.8 12.0 %collective-permute-start = (bf16[2,1,32,320]{3,2,1,0:T(8,128)(2,1)S(1)}, bf16[2,1,32,320]{3,2,1,0:T(8,128)(2,1)S(1)}, u32[]{:S(2)}, u32[]{:S(2)}) collective-permute-start(bf16[2,1,32,320]{3,2,1,0:T(8,128)(2,1)S(1)} %get-tuple-element.59), channel_id=1, source_target_pairs={{0,32},{32,64},{64,96},{96,128},{128,160},{160,192},{192,224},{1,3... | collective-permute-start | bytes 122888 | tf_op jit(solution)/shard_map/ppermute | solution.py:21
  88.9 7.0 %collective-permute-start.1 = (bf16[2,1,32,320]{3,2,1,0:T(8,128)(2,1)S(1)}, bf16[2,1,32,320]{3,2,1,0:T(8,128)(2,1)S(1)}, u32[]{:S(2)}, u32[]{:S(2)}) collective-permute-start(bf16[2,1,32,320]{3,2,1,0:T(8,128)(2,1)S(1)} %get-tuple-element.60), channel_id=1, source_target_pairs={{32,0},{64,32},{96,64},{128,96},{160,128},{192,160},{224,192},{33,... | collective-permute-start | bytes 122888 | tf_op jit(solution)/shard_map/ppermute | solution.py:23
  96.2 7.7 %collective-permute-start.2 = (bf16[2,66,1,320]{3,2,1,0:T(2,128)(2,1)S(1)}, bf16[2,66,1,320]{3,2,1,0:T(2,128)(2,1)S(1)}, u32[]{:S(2)}, u32[]{:S(2)}) collective-permute-start(bf16[2,66,1,320]{3,2,1,0:T(2,128)(2,1)S(1)} %get-tuple-element.55), channel_id=1, source_target_pairs={{0,1},{1,2},{2,3},{3,4},{4,5},{5,6},{6,7},{7,8},{8,9},{9,10},{10,1... | collective-permute-start | bytes 253448 | tf_op jit(solution)/shard_map/ppermute | solution.py:21
  101.3 10.7 %collective-permute-start.3 = (bf16[2,66,1,320]{3,2,1,0:T(2,128)(2,1)S(1)}, bf16[2,66,1,320]{3,2,1,0:T(2,128)(2,1)S(1)}, u32[]{:S(2)}, u32[]{:S(2)}) collective-permute-start(bf16[2,66,1,320]{3,2,1,0:T(2,128)(2,1)S(1)} %get-tuple-element.56), channel_id=1, source_target_pairs={{1,0},{2,1},{3,2},{4,3},{5,4},{6,5},{7,6},{8,7},{9,8},{10,9},{11,1... | collective-permute-start | bytes 253448 | tf_op jit(solution)/shard_map/ppermute | solution.py:23
  117.0 22.3 %copy-start.5 = (bf16[8,1,10,34,320]{4,3,2,1,0:T(8,128)(2,1)S(1)}, bf16[8,1,10,34,320]{4,3,2,1,0:T(8,128)(2,1)}, u32[]{:S(2)}) copy-start(bf16[8,1,10,34,320]{4,3,2,1,0:T(8,128)(2,1)} %pad_bitcast_fusion) | copy-start | bytes 5222404
  117.2 1.4 copy-start.9
  118.6 1.5 copy-start.10
  157.2 139.2 %collective-permute-start.4 = (bf16[4,3,10,34,320]{4,0,3,2,1:T(4,128)(2,1)}, bf16[4,3,10,34,320]{4,0,3,2,1:T(4,128)(2,1)}, u32[]{:S(2)}, u32[]{:S(2)}) collective-permute-start(bf16[4,3,10,34,320]{4,0,3,2,1:T(4,128)(2,1)} %copy.29), channel_id=1, source_target_pairs={{0,16},{1,17},{2,18},{3,19},{4,20},{5,21},{6,22},{7,23},{8,24},{9,... | collective-permute-start | bytes 7833608 | tf_op jit(solution)/shard_map/ppermute | solution.py:33
  315.7 1.8 copy-start.4
  317.5 1.6 copy-start.11
  325.3 1.8 copy-start.14
  340.7 1.6 copy-start.12
  344.0 1.3 copy-start.8
  354.4 1.4 copy-start.6
  354.6 1.0 copy-start.7
  357.0 61.9 %collective-permute-start.5 = (bf16[4,2,8,32,320]{4,3,2,1,0:T(8,128)(2,1)S(1)}, bf16[4,2,8,32,320]{4,3,2,1,0:T(8,128)(2,1)}, u32[]{:S(2)}, u32[]{:S(2)}) collective-permute-start(bf16[4,2,8,32,320]{4,3,2,1,0:T(8,128)(2,1)S(1)} %broadcast_select_fusion.4), channel_id=1, source_target_pairs={{0,16},{1,17},{2,18},{3,19},{4,20},{5,21},{6,22},{7,23},{8,24},{9,... | collective-permute-start | bytes 3932168 | tf_op jit(solution)/shard_map/ppermute | solution.py:33
  426.3 1.4 copy-start.1
  426.3 1.9 copy-start.3
where the time goes:
time: 433 us; the launch traced here: 431 us
  waiting for transfers between devices  199 us (46%)
  local copies, waits for them, and re-layouts  81.1 us (19%)
  blocking collectives  73.5 us (17%)
  other arithmetic  46.7 us (11%)
  starting transfers between devices  16.2 us (4%)
  matrix products  12.4 us (3%)
    ppermute x2, waiting for transfers between devices, from_partner(): return lax.ppermute(value, axis, pairs)  190 us
    psum x1, blocking collectives, per_device(): totals = lax.psum(partial_sums, ('row', 'col'))  73.5 us
    scatter x1, local copies, waits for them, and re-layouts, per_device(): first_windows.at[:, 1:-1, 1:-1]  19.2 us
    dot_general x18, matrix products, convolve(): jnp.dot(shifted, weight[tap_index], preferred_element_type=jnp.float32)  12.4 us
    scatter x1, local copies, waits for them, and re-layouts, refresh_strips(): window_two = work[:, 1].at[:, 1:-1, 1:-1].set(second)  12.2 us
    ppermute x2, starting transfers between devices, with_halo(): lax.ppermute(tail, axis, [(i, (i + 1) % count) for i in range(ends)])  10.1 us
    unnamed x41, local copies, waits for them, and re-layouts  9.83 us
  transfers between devices with their start and end apart: 6, of which 4 were waited for; matrix products, arithmetic and copies ran while one was open for 3% of the time, Pallas kernels for 0%

commit v1 on v0

v1 whole, which is shorter than its diff:
```python
import functools

import jax
import jax.numpy as jnp
from jax import lax
from jax.experimental import pallas as pl
from jax.experimental.pallas import tpu as pltpu
from jax.sharding import PartitionSpec as P

GROUPS = 32
SH = 8
EPSILON = 1e-05
LANES = 128
EXACT = lax.Precision.HIGHEST
F32 = jnp.float32
BF16 = jnp.bfloat16


def act(values, center, half_scale):
    half = (values - center) * half_scale
    return half * jnp.tanh(half) + half


def one_hot(condition, kind=F32):
    return jnp.where(condition, 1.0, 0.0).astype(kind)


def total_wait(buffer, semaphore):
    pltpu.make_async_copy(buffer, buffer, semaphore).wait()


def margins_kernel(
    cell_count,
    shape,
    stale_in,
    stale_hid,
    gain_one,
    gain_two,
    stats_out,
    rows_out,
    cols_out,
    tiles,
    cols,
    rows_in,
    cols_in,
    corners_in,
    part,
    part_in,
    group,
    group_in,
    load_sem,
    side_send,
    side_recv,
    sum_send,
    sum_recv,
):
    n_row, n_col = shape
    row, col = lax.axis_index("row"), lax.axis_index("col")
    tile_rows, tile_cols, channels = tiles.shape[1:]
    strips = tile_rows // SH
    up, down = lax.rem(row + n_row - 1, n_row), lax.rem(row + 1, n_row)
    left, right = lax.rem(col + n_col - 1, n_col), lax.rem(col + 1, n_col)
    core, site = lax.rem(col, 2), lax.div(col, 2)
    sites = n_col // 2
    first_peers, second_peers = 2 * n_row - 1, sites - 1

    def first_peer(step):
        place = lax.rem(row * 2 + core + step, 2 * n_row)
        return lax.div(place, 2), site * 2 + lax.rem(place, 2)

    def second_peer(step):
        return row, lax.rem(site + step, sites) * 2 + core

    def signal(device):
        pl.semaphore_signal(
            barrier, inc=1, device_id=device, device_id_type=pl.DeviceIdType.MESH
        )

    loads = []
    half = tile_rows // 2
    for index, source in enumerate((stale_in, stale_hid)):
        for piece in range(2):
            span = pl.ds(piece * half, half)
            copy = pltpu.make_async_copy(
                source.at[span], tiles.at[index, span], load_sem.at[index, piece]
            )
            copy.start()
            loads.append(copy)

    barrier = pltpu.get_barrier_semaphore()

    @pl.loop(1, first_peers + 1)
    def _(step):
        signal(first_peer(step))

    @pl.loop(1, second_peers + 1)
    def _(step):
        signal(second_peer(step))

    for device in ((up, left), (up, right), (row, left), (row, right), (down, left), (down, right)):
        signal(device)

    lines = lax.broadcasted_iota(jnp.int32, (channels, LANES), 0)
    lanes = lax.rem(lax.broadcasted_iota(jnp.int32, (channels, LANES), 1), GROUPS)
    size = channels // GROUPS
    gather = one_hot(jnp.logical_and(lines >= lanes * size, lines < lanes * size + size))
    sums = []
    for index in range(2):
        zero = jnp.zeros((tile_cols, channels), F32)
        carry = (zero, zero)
        for piece in range(2):
            loads[2 * index + piece].wait()

            def add(line, carry):
                values = tiles[index, line].astype(F32)
                return carry[0] + values, carry[1] + values * values

            carry = lax.fori_loop(piece * half, (piece + 1) * half, add, carry, unroll=4)
        sums += [jnp.sum(carry[0], axis=0, keepdims=True), jnp.sum(carry[1], axis=0, keepdims=True)]
    stacked = jnp.concatenate(sums + [jnp.zeros((4, channels), F32)], axis=0)
    grouped = jnp.dot(stacked, gather, precision=EXACT, preferred_element_type=F32)
    lane_part = lax.div(lax.broadcasted_iota(jnp.int32, (8, LANES), 1), GROUPS)
    kept = jnp.where(lane_part == lax.broadcasted_iota(jnp.int32, (8, LANES), 0), grouped, 0.0)
    part[...] = jnp.broadcast_to(jnp.sum(kept, axis=0, keepdims=True), (8, LANES))

    pl.semaphore_wait(barrier, first_peers + second_peers + 6)

    def send_sums(source, target, peer, count, phase):
        @pl.loop(1, count + 1)
        def _(step):
            pltpu.make_async_remote_copy(
                src_ref=source,
                dst_ref=target.at[step - 1],
                send_sem=sum_send.at[phase],
                recv_sem=sum_recv.at[phase],
                device_id=peer(step),
                device_id_type=pl.DeviceIdType.MESH,
            ).start()

    send_sums(part, part_in, first_peer, first_peers, 0)

    block = 16
    picks = lax.broadcasted_iota(jnp.int32, (2 * block, block * tile_cols), 0)
    cells = lax.broadcasted_iota(jnp.int32, (2 * block, block * tile_cols), 1)
    wanted = jnp.where(picks < block, picks * tile_cols, (picks - block) * tile_cols + tile_cols - 1)
    select = one_hot(cells == wanted, BF16)
    for index in range(2):
        for piece in range(tile_rows // block):
            span = pl.ds(piece * block, block)
            flat = tiles[index, span].reshape(block * tile_cols, channels)
            picked = jnp.dot(select, flat, preferred_element_type=F32).astype(BF16)
            cols[0, index, span] = picked[:block]
            cols[1, index, span] = picked[block:]

    head, tail = pl.ds(0, block), pl.ds(tile_rows - block, block)
    every = slice(None)
    moves = (
        (tiles.at[:, 0], rows_in.at[1], (up, col)),
        (tiles.at[:, tile_rows - 1], rows_in.at[0], (down, col)),
        (cols.at[0], cols_in.at[1], (row, left)),
        (cols.at[1], cols_in.at[0], (row, right)),
        (cols.at[0, every, head], corners_in.at[3], (up, left)),
        (cols.at[1, every, head], corners_in.at[2], (up, right)),
        (cols.at[0, every, tail], corners_in.at[1], (down, left)),
        (cols.at[1, every, tail], corners_in.at[0], (down, right)),
    )
    copies = []
    for index, (source, target, device) in enumerate(moves):
        copy = pltpu.make_async_remote_copy(
            src_ref=source,
            dst_ref=target,
            send_sem=side_send.at[index],
            recv_sem=side_recv.at[index],
            device_id=device,
            device_id_type=pl.DeviceIdType.MESH,
        )
        copy.start()
        copies.append(copy)

    total_wait(part_in, sum_recv.at[0])
    group[...] = part[...] + jnp.sum(part_in[...], axis=0)
    send_sums(group, group_in, second_peer, second_peers, 1)
    total_wait(group_in, sum_recv.at[1])
    totals = (group[...] + jnp.sum(group_in[...], axis=0)) / cell_count
    squares = pltpu.roll(totals, LANES - GROUPS, 1)
    means = lax.rem(lane_part, 2) == 0
    spread = lax.rsqrt(jnp.where(means, squares - totals * totals, 1.0) + EPSILON)
    lead = lax.broadcasted_iota(jnp.int32, (8, LANES), 0) == 0
    packed = jnp.where(lead, totals, spread)
    groups = lax.broadcasted_iota(jnp.int32, (LANES, channels), 0)
    members = lax.broadcasted_iota(jnp.int32, (LANES, channels), 1)
    factors = []
    for index, gain in enumerate((gain_one, gain_two)):
        own = (groups - 2 * GROUPS * index) * size
        valid = jnp.logical_and(groups >= 2 * GROUPS * index, groups < 2 * GROUPS * index + GROUPS)
        spill = one_hot(
            jnp.logical_and(valid, jnp.logical_and(members >= own, members < own + size))
        )
        spilt = jnp.dot(packed, spill, precision=EXACT, preferred_element_type=F32)
        factors.append((spilt[0:1], spilt[1:2] * gain[...] * 0.5))
    stats_out[...] = jnp.concatenate(
        [factors[0][0], factors[0][1], factors[1][0], factors[1][1], jnp.zeros((4, channels), F32)],
        axis=0,
    )

    for copy in copies:
        copy.wait_recv()

    outside_rows = (row == 0, row == n_row - 1)
    outside_cols = (col == 0, col == n_col - 1)
    for index, (center, scale) in enumerate(factors):

        def inner(strip, carry):
            above = tiles[index, strip * SH - 1].astype(F32)
            below = tiles[index, strip * SH].astype(F32)
            rows_out[index, 0, strip] = act(above, center, scale).astype(BF16)
            rows_out[index, 1, strip - 1] = act(below, center, scale).astype(BF16)
            return carry

        lax.fori_loop(1, strips, inner, 0)
        for side in range(2):
            value = act(rows_in[side, index].astype(F32), center, scale)
            value = jnp.where(outside_rows[side], 0.0, value)
            rows_out[index, side, side * (strips - 1)] = value.astype(BF16)
            value = act(cols_in[side, index].astype(F32), center, scale)
            value = jnp.where(outside_cols[side], 0.0, value)
            cols_out[index, side, 1 : tile_rows + 1] = value
            for end in range(2):
                value = act(corners_in[2 * end + side, index].astype(F32), center, scale)
                outside = jnp.logical_or(outside_cols[side], outside_rows[end])
                value = jnp.where(outside, 0.0, value)
                if end == 0:
                    cols_out[index, side, 0:1] = value[block - 1 : block]
                else:
                    cols_out[index, side, tile_rows + 1 : tile_rows + 2] = value[0:1]

    for copy in copies:
        copy.wait_send()
    total_wait(part_in, sum_send.at[0])
    total_wait(group_in, sum_send.at[1])


def margins(latent_shape, shape, stale_in, stale_hid, gain_one, gain_two):
    tile_rows, tile_cols, channels = latent_shape
    n_row, n_col = shape
    strips = tile_rows // SH
    cell_count = float(tile_rows * tile_cols * n_row * n_col * (channels // GROUPS))
    anywhere = pl.BlockSpec(memory_space=pl.ANY)
    vmem = pl.BlockSpec(memory_space=pltpu.VMEM)
    return pl.pallas_call(
        functools.partial(margins_kernel, cell_count, shape),
        out_shape=(
            jax.ShapeDtypeStruct((8, channels), F32),
            jax.ShapeDtypeStruct((2, 2, strips, tile_cols, channels), BF16),
            jax.ShapeDtypeStruct((2, 2, tile_rows + 16, channels), F32),
        ),
        in_specs=[anywhere, anywhere, vmem, vmem],
        out_specs=(vmem, vmem, vmem),
        scratch_shapes=[
            pltpu.VMEM((2, tile_rows, tile_cols, channels), BF16),
            pltpu.VMEM((2, 2, tile_rows, channels), BF16),
            pltpu.VMEM((2, 2, tile_cols, channels), BF16),
            pltpu.VMEM((2, 2, tile_rows, channels), BF16),
            pltpu.VMEM((4, 2, 16, channels), BF16),
            pltpu.VMEM((8, LANES), F32),
            pltpu.VMEM((2 * n_row - 1, 8, LANES), F32),
            pltpu.VMEM((8, LANES), F32),
            pltpu.VMEM((n_col // 2 - 1, 8, LANES), F32),
            pltpu.SemaphoreType.DMA((2, 2)),
            pltpu.SemaphoreType.DMA((8,)),
            pltpu.SemaphoreType.DMA((8,)),
            pltpu.SemaphoreType.DMA((2,)),
            pltpu.SemaphoreType.DMA((2,)),
        ],
        compiler_params=pltpu.CompilerParams(
            collective_id=0, has_side_effects=True, vmem_limit_bytes=24 * 2**20
        ),
        name="margins",
    )(stale_in, stale_hid, gain_one, gain_two)


def strips_kernel(
    refresh,
    stats,
    rows,
    cols,
    shift,
    latent,
    stale_hid,
    weight_one,
    weight_two,
    block_out,
    hidden_out,
    tile,
    weights,
    frame,
    window,
    hidden,
    finished,
    load_sem,
    store_sem,
):
    tile_rows, tile_cols, channels = tile.shape
    strips = tile_rows // SH
    loads = [pltpu.make_async_copy(latent, tile, load_sem.at[0])]
    for index, source in enumerate((weight_one, weight_two)):
        loads.append(
            pltpu.make_async_copy(
                source, weights.at[index, :, pl.ds(0, channels)], load_sem.at[1 + index]
            )
        )
    for copy in loads:
        copy.start()
    wide = weights.shape[2]
    weights[:, :, channels:] = jnp.zeros(weights.shape[:2] + (wide - channels, channels), BF16)
    window[:, :, :, channels:] = jnp.zeros(window.shape[:3] + (wide - channels,), BF16)
    for copy in loads:
        copy.wait()

    def convolve(index, strip, inner):
        frame[0, 8 : tile_cols + 8] = rows[index, 0, strip].astype(F32)
        frame[SH + 1, 8 : tile_cols + 8] = rows[index, 1, strip].astype(F32)
        frame[1 : SH + 1, 8 : tile_cols + 8] = inner
        for line in range(SH + 2):
            place = pl.ds(strip * SH + line, 1)
            frame[line, 7:8] = cols[index, 0, place]
            frame[line, tile_cols + 8 : tile_cols + 9] = cols[index, 1, place]
        for offset in range(3):
            window[offset, :, :, :channels] = frame[:, 7 + offset : 7 + offset + tile_cols].astype(
                BF16
            )
        taps = [
            window[tap % 3, tap // 3 : tap // 3 + SH].reshape(SH * tile_cols, wide)
            for tap in range(9)
        ]
        return jnp.dot(
            jnp.concatenate(taps, axis=1),
            weights[index].reshape(9 * wide, channels),
            preferred_element_type=F32,
        )

    def one_strip(strip, carry):
        span = pl.ds(strip * SH, SH)
        base = tile[span].astype(F32)
        first = convolve(0, strip, act(base, stats[0:1], stats[1:2]))
        fresh = (first + shift[...]).astype(BF16).reshape(SH, tile_cols, channels)
        hidden[span] = fresh
        second = convolve(1, strip, act(fresh.astype(F32), stats[2:3], stats[3:4]))
        done = tile[span].astype(F32) + second.reshape(SH, tile_cols, channels)
        finished[span] = done.astype(BF16)
        live = refresh[strip, 0] > 0

        @pl.when(live)
        def _():
            pltpu.make_async_copy(hidden.at[span], hidden_out.at[span], store_sem.at[0]).start()
            pltpu.make_async_copy(finished.at[span], block_out.at[span], store_sem.at[1]).start()

        @pl.when(jnp.logical_not(live))
        def _():
            pltpu.make_async_copy(stale_hid.at[span], hidden_out.at[span], store_sem.at[0]).start()
            pltpu.make_async_copy(tile.at[span], block_out.at[span], store_sem.at[1]).start()

        return carry

    lax.fori_loop(0, strips, one_strip, 0)
    total_wait(hidden, store_sem.at[0])
    total_wait(finished, store_sem.at[1])


def refreshed(refresh, stats, rows, cols, shift, latent, stale_hid, weight_one, weight_two):
    tile_rows, tile_cols, channels = latent.shape
    wide = -(-channels // LANES) * LANES
    anywhere = pl.BlockSpec(memory_space=pl.ANY)
    vmem = pl.BlockSpec(memory_space=pltpu.VMEM)
    tile = jax.ShapeDtypeStruct(latent.shape, BF16)
    return pl.pallas_call(
        strips_kernel,
        out_shape=(tile, tile),
        in_specs=[pl.BlockSpec(memory_space=pltpu.SMEM)] + [vmem] * 4 + [anywhere] * 4,
        out_specs=(anywhere, anywhere),
        scratch_shapes=[
            pltpu.VMEM(latent.shape, BF16),
            pltpu.VMEM((2, 9, wide, channels), BF16),
            pltpu.VMEM((SH + 2, tile_cols + 16, channels), F32),
            pltpu.VMEM((3, SH + 2, tile_cols, wide), BF16),
            pltpu.VMEM(latent.shape, BF16),
            pltpu.VMEM(latent.shape, BF16),
            pltpu.SemaphoreType.DMA((3,)),
            pltpu.SemaphoreType.DMA((2,)),
        ],
        compiler_params=pltpu.CompilerParams(vmem_limit_bytes=48 * 2**20),
        name="strips",
    )(refresh, stats, rows, cols, shift, latent, stale_hid, weight_one, weight_two)


def per_device(
    shape,
    latent,
    stale_input,
    stale_hidden,
    refresh,
    gain_one,
    weight_one,
    time_shift,
    gain_two,
    weight_two,
):
    stats, rows, cols = margins(
        latent.shape, shape, stale_input, stale_hidden, gain_one[None], gain_two[None]
    )
    return refreshed(
        refresh, stats, rows, cols, time_shift[None], latent, stale_hidden, weight_one, weight_two
    )


def solution(mesh):
    placed = (
        P("row", "col", None),
        P("row", "col", None),
        P("row", "col", None),
        P("row", "col"),
        P(),
        P(),
        P(),
        P(),
        P(),
    )
    return jax.shard_map(
        functools.partial(per_device, (mesh.shape["row"], mesh.shape["col"])),
        mesh=mesh,
        in_specs=placed,
        out_specs=(P("row", "col", None), P("row", "col", None)),
        check_vma=False,
    )
```

time: 433 us -> 52.7 us (0.12)
  the two profiles are of different devices: /device:TPU:125 before, /device:TPU:1 now
where the time goes in v1:
time: 52.7 us; the launch traced here: 52.5 us
  Pallas kernels  46.2 us (88%)
  local copies, waits for them, and re-layouts  5.6 us (11%)
  between operations  0.66 us (1%)
    pallas_call x1, Pallas kernels, margins(): pl.pallas_call(functools.partial(margins_kernel, cell_count, shape), out_...  23.2 us
    pallas_call x1, Pallas kernels, refreshed(): pl.pallas_call(strips_kernel, out_shape=(tile, tile), in_specs=[pl.BlockS...  23 us
    unnamed x9, local copies, waits for them, and re-layouts  3.55 us

profile of v1, /device:TPU:1, one launch (start us, length us, event | category | flops | bytes accessed | tf_op | source)
XLA Modules:
  0.0 52.5 jit_solution(184175290104627416)
XLA Ops:
  0.6 0.7 %broadcast_in_dim.9.gain_one = f32[1,320]{1,0:T(1,128)S(1)} reshape(f32[320]{0:T(512)} %param.13) | data formatting | bytes 2560 | tf_op jit(solution)/shard_map/broadcast_in_dim | solution.py:409
  1.3 0.7 %broadcast_in_dim.11.shift = f32[1,320]{1,0:T(1,128)S(1)} reshape(f32[320]{0:T(512)} %param.15) | data formatting | bytes 2560 | tf_op jit(solution)/shard_map/broadcast_in_dim | solution.py:412
  2.0 0.7 %broadcast_in_dim.10.gain_two = f32[1,320]{1,0:T(1,128)S(1)} reshape(f32[320]{0:T(512)} %param.16) | data formatting | bytes 2560 | tf_op jit(solution)/shard_map/broadcast_in_dim | solution.py:409
  2.7 0.7 %copy.11.refresh = s32[8,1]{1,0:T(8,128)S(1)} copy(s32[8,1]{0,1:T(1,128)} %param.12) | data formatting | bytes 64 | tf_op args[3]
  3.4 0.0 copy-start
  3.4 1.4 %copy-done = bf16[64,32,320]{2,1,0:T(8,128)(2,1)S(1)} copy-done((bf16[64,32,320]{2,1,0:T(8,128)(2,1)S(1)}, bf16[64,32,320]{2,1,0:T(8,128)(2,1)}, u32[]{:S(2)}) %copy-start) | copy-done | bytes 1310744
  4.8 0.0 copy-start.3
  4.8 1.4 %copy-done.3 = bf16[64,32,320]{2,1,0:T(8,128)(2,1)S(1)} copy-done((bf16[64,32,320]{2,1,0:T(8,128)(2,1)S(1)}, bf16[64,32,320]{2,1,0:T(8,128)(2,1)}, u32[]{:S(2)}) %copy-start.3) | copy-done | bytes 1310744
  6.2 0.0 copy-start.1
  6.2 0.0 copy-start.2
  6.2 23.2 %margins.1 = (f32[8,320]{1,0:T(8,128)S(1)}, bf16[2,2,8,32,320]{4,3,2,1,0:T(8,128)(2,1)S(1)}, f32[2,2,80,320]{3,2,1,0:T(8,128)S(1)}) custom-call(bf16[64,32,320]{2,1,0:T(8,128)(2,1)S(1)} %copy-done.3, bf16[64,32,320]{2,1,0:T(8,128)(2,1)S(1)} %copy-done, f32[1,320]{1,0:T(1,128)S(1)} %broadcast_in_dim.9.gain_one, f32[1,320]{1,0:T(1,128)S(1)} %broadcast_in_dim.10.gain_two), custom_call_target="tpu_custom_call" | custom-call | tf_op jit(solution)/shard_map/margins/pallas_call | solution.py:250
  29.4 0.0 copy-done.1
  29.4 0.0 copy-done.2
  29.4 23.0 %strips.1 = (bf16[64,32,320]{2,1,0:T(8,128)(2,1)}, bf16[64,32,320]{2,1,0:T(8,128)(2,1)}) custom-call(s32[8,1]{1,0:T(8,128)S(1)} %copy.11.refresh, f32[8,320]{1,0:T(8,128)S(1)} %get-tuple-element.5.stats, bf16[2,2,8,32,320]{4,3,2,1,0:T(8,128)(2,1)S(1)} %get-tuple-element.6.rows, f32[2,2,80,320]{3,2,1,0:T(8,128)S(1)} %get-tuple-element.7.cols, ...), custom_call_target="tpu_custom_call" | custom-call | tf_op jit(solution)/shard_map/strips/pallas_call | solution.py:376
Async XLA Ops:
  3.4 1.4 %copy-start = (bf16[64,32,320]{2,1,0:T(8,128)(2,1)S(1)}, bf16[64,32,320]{2,1,0:T(8,128)(2,1)}, u32[]{:S(2)}) copy-start(bf16[64,32,320]{2,1,0:T(8,128)(2,1)} %stale_hid.3) | copy-start | bytes 3932164
  4.8 1.4 %copy-start.3 = (bf16[64,32,320]{2,1,0:T(8,128)(2,1)S(1)}, bf16[64,32,320]{2,1,0:T(8,128)(2,1)}, u32[]{:S(2)}) copy-start(bf16[64,32,320]{2,1,0:T(8,128)(2,1)} %stale_in.1) | copy-start | bytes 3932164
  6.2 23.2 %copy-start.1 = (bf16[64,32,320]{2,1,0:T(8,128)(2,1)S(1)}, bf16[64,32,320]{2,1,0:T(8,128)(2,1)}, u32[]{:S(2)}) copy-start(bf16[64,32,320]{2,1,0:T(8,128)(2,1)} %stale_hid.3) | copy-start | bytes 3932164
  6.2 23.2 %copy-start.2 = (bf16[64,32,320]{2,1,0:T(8,128)(2,1)S(1)}, bf16[64,32,320]{2,1,0:T(8,128)(2,1)}, u32[]{:S(2)}) copy-start(bf16[64,32,320]{2,1,0:T(8,128)(2,1)} %latent.1) | copy-start | bytes 3932164

commit v2 on v1

v2 whole, which is shorter than its diff:
```python
import functools

import jax
import jax.numpy as jnp
from jax import lax
from jax.experimental import pallas as pl
from jax.experimental.pallas import tpu as pltpu
from jax.sharding import PartitionSpec as P

GROUPS = 32
SH = 8
EPSILON = 1e-05
LANES = 128
EXACT = lax.Precision.HIGHEST
F32 = jnp.float32
BF16 = jnp.bfloat16
MAIN = 256
AHEAD = 4
DEPTH = 1


def act(values, center, half_scale):
    half = (values - center) * half_scale
    return half * jnp.tanh(half) + half


def one_hot(condition, kind=F32):
    return jnp.where(condition, 1.0, 0.0).astype(kind)


def total_wait(buffer, semaphore):
    pltpu.make_async_copy(buffer, buffer, semaphore).wait()


def tails(values):
    rest = values[..., MAIN:]
    blank = jnp.zeros(rest.shape[:-1] + (LANES - rest.shape[-1],), rest.dtype)
    return jnp.concatenate([rest, blank], axis=-1)


def side_by_side(main, rest):
    turned = pltpu.roll(rest[1], LANES // 2, rest[1].ndim - 1)
    pairs = (rest[0] + turned).astype(BF16)
    return jnp.concatenate([*main, pairs, rest[2].astype(BF16)], axis=-1)


def margins_kernel(
    cell_count,
    shape,
    stale_in,
    stale_hid,
    latent,
    weight_one,
    weight_two,
    gain_one,
    gain_two,
    stats_out,
    rows_out,
    cols_out,
    tile_out,
    first_weights,
    second_weights,
    first_gain,
    second_gain,
    tiles,
    laid_out,
    raw,
    cols,
    rows_in,
    cols_in,
    corners_in,
    part,
    part_in,
    group,
    group_in,
    load_sem,
    late_sem,
    leave_sem,
    side_send,
    side_recv,
    sum_send,
    sum_recv,
):
    n_row, n_col = shape
    row, col = lax.axis_index("row"), lax.axis_index("col")
    tile_rows, tile_cols, channels = tiles.shape[1:]
    strips = tile_rows // SH
    up, down = lax.rem(row + n_row - 1, n_row), lax.rem(row + 1, n_row)
    left, right = lax.rem(col + n_col - 1, n_col), lax.rem(col + 1, n_col)
    core, x_high, z = lax.rem(col, 2), lax.rem(lax.div(col, 2), 2), lax.div(col, 4)
    y, x = lax.rem(row, 4), x_high * 2 + lax.div(row, 4)
    deep = n_col // 4
    first_peers, second_peers = 2 * deep - 1, 2 * n_row - 1

    def first_peer(step):
        place = lax.rem(z * 2 + core + lax.rem(step + deep - 1, first_peers) + 1, 2 * deep)
        return row, lax.div(place, 2) * 4 + x_high * 2 + lax.rem(place, 2)

    def second_peer(step):
        offset = lax.rem(step + 9, second_peers) + 1
        there_x, there_y = lax.rem(x + lax.div(offset, 4), 4), lax.rem(y + lax.rem(offset, 4), 4)
        there_row = lax.rem(there_x, 2) * 4 + there_y
        return there_row, z * 4 + lax.div(there_x, 2) * 2 + core

    def signal(device):
        pl.semaphore_signal(
            barrier, inc=1, device_id=device, device_id_type=pl.DeviceIdType.MESH
        )

    loads = []
    half = tile_rows // 2
    for index, source in enumerate((stale_in, stale_hid)):
        for piece in range(2):
            span = pl.ds(piece * half, half)
            copy = pltpu.make_async_copy(
                source.at[span], tiles.at[index, span], load_sem.at[index, piece]
            )
            copy.start()
            loads.append(copy)

    late = [
        pltpu.make_async_copy(weight_one, raw.at[0], late_sem.at[0]),
        pltpu.make_async_copy(weight_two, raw.at[1], late_sem.at[1]),
        pltpu.make_async_copy(latent, tile_out, late_sem.at[2]),
        pltpu.make_async_copy(gain_one, first_gain, late_sem.at[3]),
        pltpu.make_async_copy(gain_two, second_gain, late_sem.at[4]),
    ]
    for copy in late:
        copy.start()

    barrier = pltpu.get_barrier_semaphore()

    @pl.loop(0, first_peers)
    def _(step):
        signal(first_peer(step))
        signal(second_peer(step))

    for place in (up, row, down):
        for device in ((place, left), (place, right)):
            signal(device)
    signal((up, col))
    signal((down, col))

    lines = lax.broadcasted_iota(jnp.int32, (channels, LANES), 0)
    lanes = lax.rem(lax.broadcasted_iota(jnp.int32, (channels, LANES), 1), GROUPS)
    size = channels // GROUPS
    gather = one_hot(jnp.logical_and(lines >= lanes * size, lines < lanes * size + size))
    sums = []
    for index in range(2):
        zero = jnp.zeros((tile_cols, channels), F32)
        carry = (zero, zero)
        for piece in range(2):
            loads[2 * index + piece].wait()

            def add(line, carry):
                values = tiles[index, line].astype(F32)
                return carry[0] + values, carry[1] + values * values

            carry = lax.fori_loop(piece * half, (piece + 1) * half, add, carry, unroll=4)
        sums += [jnp.sum(carry[0], axis=0, keepdims=True), jnp.sum(carry[1], axis=0, keepdims=True)]
    stacked = jnp.concatenate(sums + [jnp.zeros((4, channels), F32)], axis=0)
    grouped = jnp.dot(stacked, gather, precision=EXACT, preferred_element_type=F32)
    lane_part = lax.div(lax.broadcasted_iota(jnp.int32, (8, LANES), 1), GROUPS)
    kept = jnp.where(lane_part == lax.broadcasted_iota(jnp.int32, (8, LANES), 0), grouped, 0.0)
    part[...] = jnp.broadcast_to(jnp.sum(kept, axis=0, keepdims=True), (8, LANES))

    pl.semaphore_wait(barrier, first_peers + second_peers + 8)

    def send_sums(source, target, peer, count, phase):
        @pl.loop(0, count)
        def _(step):
            pltpu.make_async_remote_copy(
                src_ref=source.at[0:1],
                dst_ref=target.at[step, 0:1],
                send_sem=sum_send.at[phase],
                recv_sem=sum_recv.at[phase],
                device_id=peer(step),
                device_id_type=pl.DeviceIdType.MESH,
            ).start()

    send_sums(part, part_in, first_peer, first_peers, 0)

    block = 16
    picks = lax.broadcasted_iota(jnp.int32, (2 * block, block * tile_cols), 0)
    cells = lax.broadcasted_iota(jnp.int32, (2 * block, block * tile_cols), 1)
    wanted = jnp.where(picks < block, picks * tile_cols, (picks - block) * tile_cols + tile_cols - 1)
    select = one_hot(cells == wanted, BF16)
    for index in range(2):
        for piece in range(tile_rows // block):
            span = pl.ds(piece * block, block)
            flat = tiles[index, span].reshape(block * tile_cols, channels)
            picked = jnp.dot(select, flat, preferred_element_type=F32).astype(BF16)
            cols[0, index, span] = picked[:block]
            cols[1, index, span] = picked[block:]

    head, tail = pl.ds(0, block), pl.ds(tile_rows - block, block)
    every = slice(None)
    moves = (
        (tiles.at[:, 0], rows_in.at[1], (up, col)),
        (tiles.at[:, tile_rows - 1], rows_in.at[0], (down, col)),
        (cols.at[0], cols_in.at[1], (row, left)),
        (cols.at[1], cols_in.at[0], (row, right)),
        (cols.at[0, every, head], corners_in.at[3], (up, left)),
        (cols.at[1, every, head], corners_in.at[2], (up, right)),
        (cols.at[0, every, tail], corners_in.at[1], (down, left)),
        (cols.at[1, every, tail], corners_in.at[0], (down, right)),
    )
    copies = []
    for index, (source, target, device) in enumerate(moves):
        copy = pltpu.make_async_remote_copy(
            src_ref=source,
            dst_ref=target,
            send_sem=side_send.at[index],
            recv_sem=side_recv.at[index],
            device_id=device,
            device_id_type=pl.DeviceIdType.MESH,
        )
        copy.start()
        copies.append(copy)

    leaving = []
    for index in range(2):
        late[index].wait()
        target = laid_out.at[index]
        for down_tap in range(3):
            taps = [raw[index, 3 * down_tap + across] for across in range(3)]
            rest = [tap[:, MAIN:] for tap in taps]
            blank = jnp.zeros_like(rest[0])
            ends = jnp.concatenate(rest + [blank], axis=1)
            pieces = [tap[:, :MAIN] for tap in taps] + [ends]
            for place, piece in enumerate(pieces):
                lanes = pl.ds(place * MAIN, MAIN)
                target[pl.ds(down_tap * MAIN, MAIN), lanes] = piece[:MAIN]
                spot = pl.ds(3 * MAIN + down_tap * (channels - MAIN), channels - MAIN)
                target[spot, lanes] = piece[MAIN:]
        spot = pl.ds(3 * channels, 4 * MAIN - 3 * channels)
        target[spot] = jnp.zeros((4 * MAIN - 3 * channels, 4 * MAIN), BF16)
        out = (first_weights, second_weights)[index]
        copy = pltpu.make_async_copy(target, out, leave_sem.at[index])
        copy.start()
        leaving.append(copy)
    late[2].wait()
    late[3].wait()
    late[4].wait()

    total_wait(part_in.at[:, 0:1], sum_recv.at[0])
    group[0:1] = part[0:1] + jnp.sum(part_in[:, 0:1], axis=0)
    send_sums(group, group_in, second_peer, second_peers, 1)
    total_wait(group_in.at[:, 0:1], sum_recv.at[1])
    totals = jnp.broadcast_to(group[0:1] + jnp.sum(group_in[:, 0:1], axis=0), (8, LANES)) / cell_count
    squares = pltpu.roll(totals, LANES - GROUPS, 1)
    means = lax.rem(lane_part, 2) == 0
    spread = lax.rsqrt(jnp.where(means, squares - totals * totals, 1.0) + EPSILON)
    lead = lax.broadcasted_iota(jnp.int32, (8, LANES), 0) == 0
    packed = jnp.where(lead, totals, spread)
    groups = lax.broadcasted_iota(jnp.int32, (LANES, channels), 0)
    members = lax.broadcasted_iota(jnp.int32, (LANES, channels), 1)
    factors = []
    for index, gain in enumerate((first_gain, second_gain)):
        own = (groups - 2 * GROUPS * index) * size
        valid = jnp.logical_and(groups >= 2 * GROUPS * index, groups < 2 * GROUPS * index + GROUPS)
        spill = one_hot(
            jnp.logical_and(valid, jnp.logical_and(members >= own, members < own + size))
        )
        spilt = jnp.dot(packed, spill, precision=EXACT, preferred_element_type=F32)
        factors.append((spilt[0:1], spilt[1:2] * gain[...].reshape(1, channels) * 0.5))
    stats_out[...] = jnp.concatenate(
        [factors[0][0], factors[0][1], factors[1][0], factors[1][1], jnp.zeros((4, channels), F32)],
        axis=0,
    )

    for copy in copies:
        copy.wait_recv()

    outside_rows = (row == 0, row == n_row - 1)
    outside_cols = (col == 0, col == n_col - 1)
    for index, (center, scale) in enumerate(factors):

        def inner(strip, carry):
            above = tiles[index, strip * SH - 1].astype(F32)
            below = tiles[index, strip * SH].astype(F32)
            rows_out[index, 0, strip] = act(above, center, scale).astype(BF16)
            rows_out[index, 1, strip - 1] = act(below, center, scale).astype(BF16)
            return carry

        lax.fori_loop(1, strips, inner, 0)
        for side in range(2):
            value = act(rows_in[side, index].astype(F32), center, scale)
            value = jnp.where(outside_rows[side], 0.0, value)
            rows_out[index, side, side * (strips - 1)] = value.astype(BF16)
            value = act(cols_in[side, index].astype(F32), center, scale)
            value = jnp.where(outside_cols[side], 0.0, value)
            cols_out[index, side, 1 : tile_rows + 1] = value
            for end in range(2):
                value = act(corners_in[2 * end + side, index].astype(F32), center, scale)
                outside = jnp.logical_or(outside_cols[side], outside_rows[end])
                value = jnp.where(outside, 0.0, value)
                if end == 0:
                    cols_out[index, side, 0:1] = value[block - 1 : block]
                else:
                    cols_out[index, side, tile_rows + 1 : tile_rows + 2] = value[0:1]

    for copy in leaving:
        copy.wait()
    for copy in copies:
        copy.wait_send()
    total_wait(part_in.at[:, 0:1], sum_send.at[0])
    total_wait(group_in.at[:, 0:1], sum_send.at[1])


def margins(shape, stale_in, stale_hid, latent, weight_one, weight_two, gain_one, gain_two):
    tile_rows, tile_cols, channels = latent.shape
    n_row, n_col = shape
    strips = tile_rows // SH
    cell_count = float(tile_rows * tile_cols * n_row * n_col * (channels // GROUPS))
    hbm = pl.BlockSpec(memory_space=pltpu.HBM)
    vmem = pl.BlockSpec(memory_space=pltpu.VMEM)
    return pl.pallas_call(
        functools.partial(margins_kernel, cell_count, shape),
        out_shape=(
            jax.ShapeDtypeStruct((8, channels), F32),
            jax.ShapeDtypeStruct((2, 2, strips, tile_cols, channels), BF16),
            jax.ShapeDtypeStruct((2, 2, tile_rows + 16, channels), F32),
            jax.ShapeDtypeStruct((tile_rows, tile_cols, channels), BF16),
            jax.ShapeDtypeStruct((4 * MAIN, 4 * MAIN), BF16),
            jax.ShapeDtypeStruct((4 * MAIN, 4 * MAIN), BF16),
        ),
        in_specs=[hbm] * 7,
        out_specs=(vmem,) * 4 + (hbm,) * 2,
        scratch_shapes=[
            pltpu.VMEM((channels,), F32),
            pltpu.VMEM((channels,), F32),
            pltpu.VMEM((2, tile_rows, tile_cols, channels), BF16),
            pltpu.VMEM((2, 4 * MAIN, 4 * MAIN), BF16),
            pltpu.VMEM((2,) + weight_one.shape, BF16),
            pltpu.VMEM((2, 2, tile_rows, channels), BF16),
            pltpu.VMEM((2, 2, tile_cols, channels), BF16),
            pltpu.VMEM((2, 2, tile_rows, channels), BF16),
            pltpu.VMEM((4, 2, 16, channels), BF16),
            pltpu.VMEM((8, LANES), F32),
            pltpu.VMEM((n_col // 2 - 1, 8, LANES), F32),
            pltpu.VMEM((8, LANES), F32),
            pltpu.VMEM((2 * n_row - 1, 8, LANES), F32),
            pltpu.SemaphoreType.DMA((2, 2)),
            pltpu.SemaphoreType.DMA((5,)),
            pltpu.SemaphoreType.DMA((2,)),
            pltpu.SemaphoreType.DMA((8,)),
            pltpu.SemaphoreType.DMA((8,)),
            pltpu.SemaphoreType.DMA((2,)),
            pltpu.SemaphoreType.DMA((2,)),
        ],
        compiler_params=pltpu.CompilerParams(
            collective_id=0, has_side_effects=True, vmem_limit_bytes=50 * 2**20
        ),
        name="margins",
    )(stale_in, stale_hid, latent, weight_one, weight_two, gain_one, gain_two)


def strips_kernel(
    refresh,
    stats,
    rows,
    cols,
    shift,
    tile,
    far_first,
    far_second,
    far_hidden,
    block_out,
    hidden_out,
    first_weights,
    second_weights,
    stale_hid,
    sides,
    hidden,
    finished,
    load_sem,
    store_sem,
):
    tile_rows, tile_cols, channels = tile.shape
    strips = tile_rows // SH
    cells = SH * tile_cols
    packs = cells // 8
    apart = tile_cols // 8
    loads = [
        pltpu.make_async_copy(far_first, first_weights, load_sem.at[0]),
        pltpu.make_async_copy(far_second, second_weights, load_sem.at[1]),
        pltpu.make_async_copy(far_hidden, stale_hid, load_sem.at[2]),
    ]
    for copy in loads:
        copy.start()
    weights = (first_weights, second_weights)

    def margin_terms(index):
        for side in range(2):
            parts = [cols[index, side, a : a + tile_rows] for a in range(3)]
            lhs = side_by_side([part[:, :MAIN].astype(BF16) for part in parts], [tails(part) for part in parts])
            start = 2 * MAIN * side
            sides[index, side, :, :MAIN] = jnp.dot(
                lhs, weights[index][:, start : start + MAIN], preferred_element_type=F32
            )
            start = 3 * MAIN + LANES * side
            sides[index, side, :, MAIN:] = jnp.dot(
                lhs, weights[index][:, start : start + LANES], preferred_element_type=F32
            )
    sub = lax.broadcasted_iota(jnp.int32, (1, 8, 1), 1)

    def moved(index, side, strip, part, lanes):
        width = part.shape[-1]
        turned = pltpu.roll(part.reshape(packs, 8, width), 1 if side == 0 else 7, 1)
        pieces = []
        for line in range(SH):
            edge = jnp.broadcast_to(
                sides[index, side, strip * SH + line : strip * SH + line + 1, lanes], (8, width)
            )[None]
            first = line * apart
            if side == 0:
                pieces += [edge, turned[first : first + apart - 1]]
            else:
                pieces += [turned[first + 1 : first + apart], edge]
        carried = jnp.concatenate(pieces, axis=0)
        at = 0 if side == 0 else 7
        return jnp.where(sub == at, carried, turned).reshape(cells, width)

    def multiply(index, strip, inner):
        above, below = rows[index, 0, strip].astype(F32), rows[index, 1, strip].astype(F32)
        values = jnp.concatenate([above[None], inner, below[None]], axis=0)
        main = values[..., :MAIN].astype(BF16)
        rest = tails(values)
        wide = side_by_side(
            [main[a : a + SH] for a in range(3)], [rest[a : a + SH] for a in range(3)]
        ).reshape(cells, 4 * MAIN)
        return [
            jnp.dot(
                wide,
                weights[index][:, part * MAIN : (part + 1) * MAIN],
                preferred_element_type=F32,
            )
            for part in range(4)
        ]

    def collect(index, strip, products):
        early, same, late, rest = products
        low, high = slice(0, MAIN), slice(MAIN, MAIN + LANES)
        main = moved(index, 0, strip, early, low) + same + moved(index, 1, strip, late, low)
        ends = (
            moved(index, 0, strip, rest[:, :LANES], high)
            + pltpu.roll(rest[:, :LANES], LANES // 2, 1)
            + moved(index, 1, strip, rest[:, LANES:], high)
        )
        return jnp.concatenate([main, ends[:, : channels - MAIN]], axis=1)

    fresh = {}

    def begin(index, strip):
        span = slice(strip * SH, strip * SH + SH)
        if index == 0:
            inner = act(tile[span].astype(F32), stats[0:1], stats[1:2])
        else:
            inner = act(fresh[strip].astype(F32), stats[2:3], stats[3:4])
        return multiply(index, strip, inner)

    def finish(index, strip, products):
        span = slice(strip * SH, strip * SH + SH)
        live = refresh[0, strip] > 0
        summed = collect(index, strip, products)
        if index == 0:
            value = (summed + shift[...].reshape(1, channels)).astype(BF16).reshape(SH, tile_cols, channels)
            fresh[strip] = value
            hidden[span] = jnp.where(live, value, stale_hid[span])
            made, out = hidden, hidden_out
        else:
            value = tile[span].astype(F32) + summed.reshape(SH, tile_cols, channels)
            finished[span] = jnp.where(live, value.astype(BF16), tile[span])
            made, out = finished, block_out
        pltpu.make_async_copy(made.at[span], out.at[span], store_sem.at[index]).start()

    loads[0].wait()
    margin_terms(0)
    jobs = [(index, strip) for half in range(0, strips, AHEAD) for index in range(2) for strip in range(half, half + AHEAD)]
    waiting, done = [], []
    for job in jobs:
        waiting.append((*job, begin(*job)))
        if len(waiting) > DEPTH:
            if len(done) == 0:
                for copy in loads[1:]:
                    copy.wait()
                margin_terms(1)
            done.append(waiting[0][:2])
            finish(*waiting.pop(0))
    for job in waiting:
        finish(*job)
    total_wait(hidden, store_sem.at[0])
    total_wait(finished, store_sem.at[1])


def refreshed(
    refresh, stats, rows, cols, shift, tile, first_weights, second_weights, stale_hid
):
    tile_shape = tile.shape
    tile_rows, tile_cols, channels = tile_shape
    anywhere = pl.BlockSpec(memory_space=pl.ANY)
    vmem = pl.BlockSpec(memory_space=pltpu.VMEM)
    out = jax.ShapeDtypeStruct(tile_shape, BF16)
    return pl.pallas_call(
        strips_kernel,
        out_shape=(out, out),
        in_specs=[pl.BlockSpec(memory_space=pltpu.SMEM)] + [vmem] * 5 + [anywhere] * 3,
        out_specs=(anywhere, anywhere),
        scratch_shapes=[
            pltpu.VMEM((4 * MAIN, 4 * MAIN), BF16),
            pltpu.VMEM((4 * MAIN, 4 * MAIN), BF16),
            pltpu.VMEM(tile_shape, BF16),
            pltpu.VMEM((2, 2, tile_rows, MAIN + LANES), F32),
            pltpu.VMEM(tile_shape, BF16),
            pltpu.VMEM(tile_shape, BF16),
            pltpu.SemaphoreType.DMA((3,)),
            pltpu.SemaphoreType.DMA((2,)),
        ],
        compiler_params=pltpu.CompilerParams(vmem_limit_bytes=50 * 2**20),
        name="strips",
    )(refresh, stats, rows, cols, shift, tile, first_weights, second_weights, stale_hid)


def per_device(
    shape,
    latent,
    stale_input,
    stale_hidden,
    refresh,
    gain_one,
    weight_one,
    time_shift,
    gain_two,
    weight_two,
):
    stats, rows, cols, tile, first_weights, second_weights = margins(
        shape, stale_input, stale_hidden, latent, weight_one, weight_two, gain_one, gain_two
    )
    return refreshed(
        refresh.T, stats, rows, cols, time_shift, tile, first_weights, second_weights, stale_hidden
    )


def solution(mesh):
    placed = (
        P("row", "col", None),
        P("row", "col", None),
        P("row", "col", None),
        P("row", "col"),
        P(),
        P(),
        P(),
        P(),
        P(),
    )
    return jax.shard_map(
        functools.partial(per_device, (mesh.shape["row"], mesh.shape["col"])),
        mesh=mesh,
        in_specs=placed,
        out_specs=(P("row", "col", None), P("row", "col", None)),
        check_vma=False,
    )
```

time: 52.7 us -> 36.7 us (0.70)
  Pallas kernels: 46.2 us -> 34.6 us
  local copies, waits for them, and re-layouts: 5.6 us -> 1.36 us
    pallas_call x1, Pallas kernels: 23 us -> 13.5 us  [refreshed(): pl.pallas_call(strips_kernel, out_shape=(out, out), in_specs=[pl.BlockSpe...]
    unnamed x9 -> x8, local copies, waits for them, and re-layouts: 3.55 us -> 1.36 us
    pallas_call x1, Pallas kernels: 23.2 us -> 21.1 us  [margins(): pl.pallas_call(functools.partial(margins_kernel, cell_count, shape), out_...]
    broadcast_in_dim x3 -> x0, local copies, waits for them, and re-layouts: 2.05 us -> none  [the longest x1 0.68 us: per_device(): gain_one[None]]
where the time goes in v2:
time: 36.7 us; the launch traced here: 36.6 us
  Pallas kernels  34.6 us (94%)
  local copies, waits for them, and re-layouts  1.36 us (4%)
  between operations  0.67 us (2%)
    pallas_call x1, Pallas kernels, margins(): pl.pallas_call(functools.partial(margins_kernel, cell_count, shape), out_...  21.1 us
    pallas_call x1, Pallas kernels, refreshed(): pl.pallas_call(strips_kernel, out_shape=(out, out), in_specs=[pl.BlockSpe...  13.5 us
    unnamed x8, local copies, waits for them, and re-layouts  1.36 us

profile of v2, /device:TPU:1, one launch (start us, length us, event | category | flops | bytes accessed | tf_op | source)
XLA Modules:
  0.0 36.6 jit_solution(10172532438496119561)
XLA Ops:
  0.6 0.0 copy-start
  0.6 0.7 %copy-done = f32[320]{0:T(512)S(1)} copy-done((f32[320]{0:T(512)S(1)}, f32[320]{0:T(512)}, u32[]{:S(2)}) %copy-start) | copy-done | bytes 1304
  1.3 0.0 copy-start.1
  1.3 0.7 %copy-done.1 = f32[320]{0:T(512)S(1)} copy-done((f32[320]{0:T(512)S(1)}, f32[320]{0:T(512)}, u32[]{:S(2)}) %copy-start.1) | copy-done | bytes 1304
  2.0 0.0 copy-start.2
  2.0 0.0 copy-start.3
  2.0 21.1 %margins.1 = (f32[8,320]{1,0:T(8,128)S(1)}, bf16[2,2,8,32,320]{4,3,2,1,0:T(8,128)(2,1)S(1)}, f32[2,2,80,320]{3,2,1,0:T(8,128)S(1)}, bf16[64,32,320]{2,1,0:T(8,12...) custom-call(bf16[64,32,320]{2,1,0:T(8,128)(2,1)} %stale_in.1, bf16[64,32,320]{2,1,0:T(8,128)(2,1)} %far_hidden.1, ...), custom_call_target="tpu_custom_call" | custom-call | tf_op jit(solution)/shard_map/margins/pallas_call | solution.py:318
  23.1 0.0 copy-done.2
  23.1 0.0 copy-done.3
  23.1 13.5 %strips.1 = (bf16[64,32,320]{2,1,0:T(8,128)(2,1)}, bf16[64,32,320]{2,1,0:T(8,128)(2,1)}) custom-call(s32[1,8]{1,0:T(1,128)S(1)} %bitcast.1, f32[8,320]{1,0:T(8,128)S(1)} %get-tuple-element.8.stats, bf16[2,2,8,32,320]{4,3,2,1,0:T(8,128)(2,1)S(1)} %get-tuple-element.9.rows, f32[2,2,80,320]{3,2,1,0:T(8,128)S(1)} %get-tuple-element.10.cols, f32[320]{0:T(512)S(1)} %copy-done.2, ...), custom_call_target="tpu_custom_call" | custom-call | tf_op jit(solution)/shard_map/strips/pallas_call | solution.py:505
Async XLA Ops:
  0.6 0.7 %copy-start = (f32[320]{0:T(512)S(1)}, f32[320]{0:T(512)}, u32[]{:S(2)}) copy-start(f32[320]{0:T(512)} %gain_one.1) | copy-start | bytes 3844
  1.3 0.7 %copy-start.1 = (f32[320]{0:T(512)S(1)}, f32[320]{0:T(512)}, u32[]{:S(2)}) copy-start(f32[320]{0:T(512)} %gain_two.1) | copy-start | bytes 3844
  2.0 21.1 %copy-start.2 = (f32[320]{0:T(512)S(1)}, f32[320]{0:T(512)}, u32[]{:S(2)}) copy-start(f32[320]{0:T(512)} %shift.1) | copy-start | bytes 3844
  2.0 21.1 %copy-start.3 = (s32[8,1]{0,1:T(1,128)S(1)}, s32[8,1]{0,1:T(1,128)}, u32[]{:S(2)}) copy-start(s32[8,1]{0,1:T(1,128)} %param.12) | copy-start | bytes 100

commit v3 on v2

--- a/solution.py
+++ b/solution.py
@@ -52,16 +52,12 @@
     latent,
     weight_one,
     weight_two,
-    gain_one,
-    gain_two,
-    stats_out,
+    totals_out,
     rows_out,
     cols_out,
     tile_out,
     first_weights,
     second_weights,
-    first_gain,
-    second_gain,
     tiles,
     laid_out,
     raw,
@@ -122,8 +118,6 @@
         pltpu.make_async_copy(weight_one, raw.at[0], late_sem.at[0]),
         pltpu.make_async_copy(weight_two, raw.at[1], late_sem.at[1]),
         pltpu.make_async_copy(latent, tile_out, late_sem.at[2]),
-        pltpu.make_async_copy(gain_one, first_gain, late_sem.at[3]),
-        pltpu.make_async_copy(gain_two, second_gain, late_sem.at[4]),
     ]
     for copy in late:
         copy.start()
@@ -240,65 +234,32 @@
         copy.start()
         leaving.append(copy)
     late[2].wait()
-    late[3].wait()
-    late[4].wait()
 
     total_wait(part_in.at[:, 0:1], sum_recv.at[0])
     group[0:1] = part[0:1] + jnp.sum(part_in[:, 0:1], axis=0)
     send_sums(group, group_in, second_peer, second_peers, 1)
-    total_wait(group_in.at[:, 0:1], sum_recv.at[1])
-    totals = jnp.broadcast_to(group[0:1] + jnp.sum(group_in[:, 0:1], axis=0), (8, LANES)) / cell_count
-    squares = pltpu.roll(totals, LANES - GROUPS, 1)
-    means = lax.rem(lane_part, 2) == 0
-    spread = lax.rsqrt(jnp.where(means, squares - totals * totals, 1.0) + EPSILON)
-    lead = lax.broadcasted_iota(jnp.int32, (8, LANES), 0) == 0
-    packed = jnp.where(lead, totals, spread)
-    groups = lax.broadcasted_iota(jnp.int32, (LANES, channels), 0)
-    members = lax.broadcasted_iota(jnp.int32, (LANES, channels), 1)
-    factors = []
-    for index, gain in enumerate((first_gain, second_gain)):
-        own = (groups - 2 * GROUPS * index) * size
-        valid = jnp.logical_and(groups >= 2 * GROUPS * index, groups < 2 * GROUPS * index + GROUPS)
-        spill = one_hot(
-            jnp.logical_and(valid, jnp.logical_and(members >= own, members < own + size))
-        )
-        spilt = jnp.dot(packed, spill, precision=EXACT, preferred_element_type=F32)
-        factors.append((spilt[0:1], spilt[1:2] * gain[...].reshape(1, channels) * 0.5))
-    stats_out[...] = jnp.concatenate(
-        [factors[0][0], factors[0][1], factors[1][0], factors[1][1], jnp.zeros((4, channels), F32)],
-        axis=0,
-    )
-
+    def inner(strip, carry):
+        for index in range(2):
+            rows_out[index, 0, strip] = tiles[index, strip * SH - 1]
+            rows_out[index, 1, strip - 1] = tiles[index, strip * SH]
+        return carry
+
+    lax.fori_loop(1, strips, inner, 0)
     for copy in copies:
         copy.wait_recv()
-
-    outside_rows = (row == 0, row == n_row - 1)
-    outside_cols = (col == 0, col == n_col - 1)
-    for index, (center, scale) in enumerate(factors):
-
-        def inner(strip, carry):
-            above = tiles[index, strip * SH - 1].astype(F32)
-            below = tiles[index, strip * SH].astype(F32)
-            rows_out[index, 0, strip] = act(above, center, scale).astype(BF16)
-            rows_out[index, 1, strip - 1] = act(below, center, scale).astype(BF16)
-            return carry
-
-        lax.fori_loop(1, strips, inner, 0)
+    for index in range(2):
         for side in range(2):
-            value = act(rows_in[side, index].astype(F32), center, scale)
-            value = jnp.where(outside_rows[side], 0.0, value)
-            rows_out[index, side, side * (strips - 1)] = value.astype(BF16)
-            value = act(cols_in[side, index].astype(F32), center, scale)
-            value = jnp.where(outside_cols[side], 0.0, value)
-            cols_out[index, side, 1 : tile_rows + 1] = value
-            for end in range(2):
-                value = act(corners_in[2 * end + side, index].astype(F32), center, scale)
-                outside = jnp.logical_or(outside_cols[side], outside_rows[end])
-                value = jnp.where(outside, 0.0, value)
-                if end == 0:
-                    cols_out[index, side, 0:1] = value[block - 1 : block]
-                else:
-                    cols_out[index, side, tile_rows + 1 : tile_rows + 2] = value[0:1]
+            rows_out[index, side, side * (strips - 1)] = rows_in[side, index]
+            cols_out[index, side, 1 : tile_rows + 1] = cols_in[side, index].astype(F32)
+            above, below = corners_in[side, index], corners_in[2 + side, index]
+            cols_out[index, side, 0:1] = above.astype(F32)[block - 1 : block]
+            cols_out[index, side, tile_rows + 1 :] = jnp.broadcast_to(
+                below.astype(F32)[0:1], (15, channels)
+            )
+
+    total_wait(group_in.at[:, 0:1], sum_recv.at[1])
+    totals = group[0:1] + jnp.sum(group_in[:, 0:1], axis=0)
+    totals_out[...] = jnp.broadcast_to(totals, (8, LANES)) / cell_count
 
     for copy in leaving:
         copy.wait()
@@ -308,7 +269,7 @@
     total_wait(group_in.at[:, 0:1], sum_send.at[1])
 
 
-def margins(shape, stale_in, stale_hid, latent, weight_one, weight_two, gain_one, gain_two):
+def margins(shape, stale_in, stale_hid, latent, weight_one, weight_two):
     tile_rows, tile_cols, channels = latent.shape
     n_row, n_col = shape
     strips = tile_rows // SH
@@ -318,18 +279,16 @@
     return pl.pallas_call(
         functools.partial(margins_kernel, cell_count, shape),
         out_shape=(
-            jax.ShapeDtypeStruct((8, channels), F32),
+            jax.ShapeDtypeStruct((8, LANES), F32),
             jax.ShapeDtypeStruct((2, 2, strips, tile_cols, channels), BF16),
             jax.ShapeDtypeStruct((2, 2, tile_rows + 16, channels), F32),
             jax.ShapeDtypeStruct((tile_rows, tile_cols, channels), BF16),
             jax.ShapeDtypeStruct((4 * MAIN, 4 * MAIN), BF16),
             jax.ShapeDtypeStruct((4 * MAIN, 4 * MAIN), BF16),
         ),
-        in_specs=[hbm] * 7,
+        in_specs=[hbm] * 5,
         out_specs=(vmem,) * 4 + (hbm,) * 2,
         scratch_shapes=[
-            pltpu.VMEM((channels,), F32),
-            pltpu.VMEM((channels,), F32),
             pltpu.VMEM((2, tile_rows, tile_cols, channels), BF16),
             pltpu.VMEM((2, 4 * MAIN, 4 * MAIN), BF16),
             pltpu.VMEM((2,) + weight_one.shape, BF16),
@@ -342,7 +301,7 @@
             pltpu.VMEM((8, LANES), F32),
             pltpu.VMEM((2 * n_row - 1, 8, LANES), F32),
             pltpu.SemaphoreType.DMA((2, 2)),
-            pltpu.SemaphoreType.DMA((5,)),
+            pltpu.SemaphoreType.DMA((3,)),
             pltpu.SemaphoreType.DMA((2,)),
             pltpu.SemaphoreType.DMA((8,)),
             pltpu.SemaphoreType.DMA((8,)),
@@ -353,12 +312,38 @@
             collective_id=0, has_side_effects=True, vmem_limit_bytes=50 * 2**20
         ),
         name="margins",
-    )(stale_in, stale_hid, latent, weight_one, weight_two, gain_one, gain_two)
+    )(stale_in, stale_hid, latent, weight_one, weight_two)
+
+
+def factors(totals, gains):
+    channels = gains[0].shape[0]
+    size = channels // GROUPS
+    squares = pltpu.roll(totals, LANES - GROUPS, 1)
+    lane_part = lax.div(lax.broadcasted_iota(jnp.int32, (8, LANES), 1), GROUPS)
+    means = lax.rem(lane_part, 2) == 0
+    spread = lax.rsqrt(jnp.where(means, squares - totals * totals, 1.0) + EPSILON)
+    lead = lax.broadcasted_iota(jnp.int32, (8, LANES), 0) == 0
+    packed = jnp.where(lead, totals, spread)
+    groups = lax.broadcasted_iota(jnp.int32, (LANES, channels), 0)
+    members = lax.broadcasted_iota(jnp.int32, (LANES, channels), 1)
+    made = []
+    for index, gain in enumerate(gains):
+        own = (groups - 2 * GROUPS * index) * size
+        valid = jnp.logical_and(groups >= 2 * GROUPS * index, groups < 2 * GROUPS * index + GROUPS)
+        spill = one_hot(
+            jnp.logical_and(valid, jnp.logical_and(members >= own, members < own + size))
+        )
+        spilt = jnp.dot(packed, spill, precision=EXACT, preferred_element_type=F32)
+        made.append((spilt[0:1], spilt[1:2] * gain[...].reshape(1, channels) * 0.5))
+    return made
 
 
 def strips_kernel(
+    shape,
     refresh,
-    stats,
+    totals,
+    gain_one,
+    gain_two,
     rows,
     cols,
     shift,
@@ -371,6 +356,7 @@
     first_weights,
     second_weights,
     stale_hid,
+    edges,
     sides,
     hidden,
     finished,
@@ -390,10 +376,25 @@
     for copy in loads:
         copy.start()
     weights = (first_weights, second_weights)
+    n_row, n_col = shape
+    row, col = lax.axis_index("row"), lax.axis_index("col")
+    outside_rows = (row == 0, row == n_row - 1)
+    outside_cols = (col == 0, col == n_col - 1)
+    stats = factors(totals[...], (gain_one, gain_two))
+    lines = lax.broadcasted_iota(jnp.int32, (cols.shape[2], 1), 0)
+    beyond = jnp.logical_or(
+        jnp.logical_and(lines == 0, outside_rows[0]),
+        jnp.logical_and(lines == tile_rows + 1, outside_rows[1]),
+    )
+    for index in range(2):
+        for side in range(2):
+            value = act(cols[index, side], *stats[index])
+            outside = jnp.logical_or(beyond, outside_cols[side])
+            edges[index, side] = jnp.where(outside, 0.0, value)
 
     def margin_terms(index):
         for side in range(2):
-            parts = [cols[index, side, a : a + tile_rows] for a in range(3)]
+            parts = [edges[index, side, a : a + tile_rows] for a in range(3)]
             lhs = side_by_side([part[:, :MAIN].astype(BF16) for part in parts], [tails(part) for part in parts])
             start = 2 * MAIN * side
             sides[index, side, :, :MAIN] = jnp.dot(
@@ -423,7 +424,13 @@
         return jnp.where(sub == at, carried, turned).reshape(cells, width)
 
     def multiply(index, strip, inner):
-        above, below = rows[index, 0, strip].astype(F32), rows[index, 1, strip].astype(F32)
+        above, below = (
+            act(rows[index, side, strip].astype(F32), *stats[index]) for side in range(2)
+        )
+        if strip == 0:
+            above = jnp.where(outside_rows[0], 0.0, above)
+        if strip == strips - 1:
+            below = jnp.where(outside_rows[1], 0.0, below)
         values = jnp.concatenate([above[None], inner, below[None]], axis=0)
         main = values[..., :MAIN].astype(BF16)
         rest = tails(values)
@@ -455,9 +462,9 @@
     def begin(index, strip):
         span = slice(strip * SH, strip * SH + SH)
         if index == 0:
-            inner = act(tile[span].astype(F32), stats[0:1], stats[1:2])
+            inner = act(tile[span].astype(F32), *stats[0])
         else:
-            inner = act(fresh[strip].astype(F32), stats[2:3], stats[3:4])
+            inner = act(fresh[strip].astype(F32), *stats[1])
         return multiply(index, strip, inner)
 
     def finish(index, strip, products):
@@ -495,7 +502,18 @@
 
 
 def refreshed(
-    refresh, stats, rows, cols, shift, tile, first_weights, second_weights, stale_hid
+    shape,
+    refresh,
+    totals,
+    gain_one,
+    gain_two,
+    rows,
+    cols,
+    shift,
+    tile,
+    first_weights,
+    second_weights,
+    stale_hid,
 ):
     tile_shape = tile.shape
     tile_rows, tile_cols, channels = tile_shape
@@ -503,14 +521,15 @@
     vmem = pl.BlockSpec(memory_space=pltpu.VMEM)
     out = jax.ShapeDtypeStruct(tile_shape, BF16)
     return pl.pallas_call(
-        strips_kernel,
+        functools.partial(strips_kernel, shape),
         out_shape=(out, out),
-        in_specs=[pl.BlockSpec(memory_space=pltpu.SMEM)] + [vmem] * 5 + [anywhere] * 3,
+        in_specs=[pl.BlockSpec(memory_space=pltpu.SMEM)] + [vmem] * 7 + [anywhere] * 3,
         out_specs=(anywhere, anywhere),
         scratch_shapes=[
             pltpu.VMEM((4 * MAIN, 4 * MAIN), BF16),
             pltpu.VMEM((4 * MAIN, 4 * MAIN), BF16),
             pltpu.VMEM(tile_shape, BF16),
+            pltpu.VMEM(cols.shape, F32),
             pltpu.VMEM((2, 2, tile_rows, MAIN + LANES), F32),
             pltpu.VMEM(tile_shape, BF16),
             pltpu.VMEM(tile_shape, BF16),
@@ -519,7 +538,19 @@
         ],
         compiler_params=pltpu.CompilerParams(vmem_limit_bytes=50 * 2**20),
         name="strips",
-    )(refresh, stats, rows, cols, shift, tile, first_weights, second_weights, stale_hid)
+    )(
+        refresh,
+        totals,
+        gain_one,
+        gain_two,
+        rows,
+        cols,
+        shift,
+        tile,
+        first_weights,
+        second_weights,
+        stale_hid,
+    )
 
 
 def per_device(
@@ -534,11 +565,22 @@
     gain_two,
     weight_two,
 ):
-    stats, rows, cols, tile, first_weights, second_weights = margins(
-        shape, stale_input, stale_hidden, latent, weight_one, weight_two, gain_one, gain_two
+    totals, rows, cols, tile, first_weights, second_weights = margins(
+        shape, stale_input, stale_hidden, latent, weight_one, weight_two
     )
     return refreshed(
-        refresh.T, stats, rows, cols, time_shift, tile, first_weights, second_weights, stale_hidden
+        shape,
+        refresh.T,
+        totals,
+        gain_one,
+        gain_two,
+        rows,
+        cols,
+        time_shift,
+        tile,
+        first_weights,
+        second_weights,
+        stale_hidden,
     )
 
 

time: 36.7 us -> 34.5 us (0.940)
  local copies, waits for them, and re-layouts: 1.36 us -> 0.02 us
  Pallas kernels: 34.6 us -> 33.7 us
    unnamed x8, local copies, waits for them, and re-layouts: 1.36 us -> 0.02 us
    pallas_call x1, Pallas kernels: 21.1 us -> 20.3 us  [margins(): pl.pallas_call(functools.partial(margins_kernel, cell_count, shape), out_...]
where the time goes in v3:
time: 34.5 us; the launch traced here: 34.4 us
  Pallas kernels  33.7 us (98%)
  between operations  0.7 us (2%)
    pallas_call x1, Pallas kernels, margins(): pl.pallas_call(functools.partial(margins_kernel, cell_count, shape), out_...  20.3 us
    pallas_call x1, Pallas kernels, refreshed(): pl.pallas_call(functools.partial(strips_kernel, shape), out_shape=(out, o...  13.5 us

profile of v3, /device:TPU:1, one launch (start us, length us, event | category | flops | bytes accessed | tf_op | source)
XLA Modules:
  0.0 34.4 jit_solution(551758564310964280)
XLA Ops:
  0.6 0.0 copy-start
  0.6 0.0 copy-start.1
  0.7 0.0 copy-start.2
  0.7 0.0 copy-start.3
  0.7 20.3 %margins.1 = (f32[8,128]{1,0:T(8,128)S(1)}, bf16[2,2,8,32,320]{4,3,2,1,0:T(8,128)(2,1)S(1)}, f32[2,2,80,320]{3,2,1,0:T(8,128)S(1)}, bf16[64,32,320]{2,1,0:T(8,12...) custom-call(bf16[64,32,320]{2,1,0:T(8,128)(2,1)} %stale_in.1, bf16[64,32,320]{2,1,0:T(8,128)(2,1)} %far_hidden.1, ...), custom_call_target="tpu_custom_call" | custom-call | tf_op jit(solution)/shard_map/margins/pallas_call | solution.py:279
  21.0 0.0 copy-done
  21.0 0.0 copy-done.1
  21.0 0.0 copy-done.2
  21.0 0.0 copy-done.3
  21.0 13.5 %strips.1 = (bf16[64,32,320]{2,1,0:T(8,128)(2,1)}, bf16[64,32,320]{2,1,0:T(8,128)(2,1)}) custom-call(s32[1,8]{1,0:T(1,128)S(1)} %bitcast.1, f32[8,128]{1,0:T(8,128)S(1)} %get-tuple-element.8.totals, f32[320]{0:T(512)S(1)} %copy-done, f32[320]{0:T(512)S(1)} %copy-done.1, bf16[2,2,8,32,320]{4,3,2,1,0:T(8,128)(2,1)S(1)} %get-tuple-element.9.rows, ...), custom_call_target="tpu_custom_call" | custom-call | tf_op jit(solution)/shard_map/strips/pallas_call | solution.py:523
Async XLA Ops:
  0.6 20.3 %copy-start = (f32[320]{0:T(512)S(1)}, f32[320]{0:T(512)}, u32[]{:S(2)}) copy-start(f32[320]{0:T(512)} %gain_one.1) | copy-start | bytes 3844
  0.6 20.3 %copy-start.1 = (f32[320]{0:T(512)S(1)}, f32[320]{0:T(512)}, u32[]{:S(2)}) copy-start(f32[320]{0:T(512)} %gain_two.1) | copy-start | bytes 3844
  0.7 20.3 %copy-start.2 = (f32[320]{0:T(512)S(1)}, f32[320]{0:T(512)}, u32[]{:S(2)}) copy-start(f32[320]{0:T(512)} %shift.1) | copy-start | bytes 3844
  0.7 20.3 %copy-start.3 = (s32[8,1]{0,1:T(1,128)S(1)}, s32[8,1]{0,1:T(1,128)}, u32[]{:S(2)}) copy-start(s32[8,1]{0,1:T(1,128)} %param.12) | copy-start | bytes 100

commit v4 on v3

--- a/solution.py
+++ b/solution.py
@@ -15,8 +15,6 @@
 F32 = jnp.float32
 BF16 = jnp.bfloat16
 MAIN = 256
-AHEAD = 4
-DEPTH = 1
 
 
 def act(values, center, half_scale):
@@ -322,19 +320,25 @@
     lane_part = lax.div(lax.broadcasted_iota(jnp.int32, (8, LANES), 1), GROUPS)
     means = lax.rem(lane_part, 2) == 0
     spread = lax.rsqrt(jnp.where(means, squares - totals * totals, 1.0) + EPSILON)
-    lead = lax.broadcasted_iota(jnp.int32, (8, LANES), 0) == 0
-    packed = jnp.where(lead, totals, spread)
     groups = lax.broadcasted_iota(jnp.int32, (LANES, channels), 0)
     members = lax.broadcasted_iota(jnp.int32, (LANES, channels), 1)
+    parts = []
+    for value in (totals[0:1], spread[0:1]):
+        for _ in range(3):
+            parts.append(value.astype(BF16).astype(F32))
+            value = value - parts[-1]
+    packed = jnp.concatenate(parts + [jnp.zeros((2, LANES), F32)], axis=0).astype(BF16)
     made = []
     for index, gain in enumerate(gains):
         own = (groups - 2 * GROUPS * index) * size
         valid = jnp.logical_and(groups >= 2 * GROUPS * index, groups < 2 * GROUPS * index + GROUPS)
         spill = one_hot(
-            jnp.logical_and(valid, jnp.logical_and(members >= own, members < own + size))
+            jnp.logical_and(valid, jnp.logical_and(members >= own, members < own + size)), BF16
         )
-        spilt = jnp.dot(packed, spill, precision=EXACT, preferred_element_type=F32)
-        made.append((spilt[0:1], spilt[1:2] * gain[...].reshape(1, channels) * 0.5))
+        spilt = jnp.dot(packed, spill, preferred_element_type=F32)
+        center = spilt[0:1] + spilt[1:2] + spilt[2:3]
+        scale = spilt[3:4] + spilt[4:5] + spilt[5:6]
+        made.append((center, scale * gain[...].reshape(1, channels) * 0.5))
     return made
 
 
@@ -356,6 +360,7 @@
     first_weights,
     second_weights,
     stale_hid,
+    order,
     edges,
     sides,
     hidden,
@@ -376,6 +381,21 @@
     for copy in loads:
         copy.start()
     weights = (first_weights, second_weights)
+    live_total = sum(refresh[0, strip] for strip in range(strips))
+    pairs = lax.div(live_total + 1, 2)
+    before = jnp.int32(0)
+    for strip in range(strips):
+        flag = refresh[0, strip]
+        order[jnp.where(flag > 0, before, live_total + strip - before)] = jnp.int32(strip)
+        before += flag
+    for place in range(strips):
+
+        @pl.when(place >= 2 * pairs)
+        def _():
+            span = pl.ds(order[place] * SH, SH)
+            pltpu.make_async_copy(far_hidden.at[span], hidden_out.at[span], store_sem.at[0]).start()
+            pltpu.make_async_copy(tile.at[span], block_out.at[span], store_sem.at[1]).start()
+
     n_row, n_col = shape
     row, col = lax.axis_index("row"), lax.axis_index("col")
     outside_rows = (row == 0, row == n_row - 1)
@@ -410,10 +430,9 @@
         width = part.shape[-1]
         turned = pltpu.roll(part.reshape(packs, 8, width), 1 if side == 0 else 7, 1)
         pieces = []
+        margin = sides[index, side, pl.ds(pl.multiple_of(strip * SH, SH), SH), lanes]
         for line in range(SH):
-            edge = jnp.broadcast_to(
-                sides[index, side, strip * SH + line : strip * SH + line + 1, lanes], (8, width)
-            )[None]
+            edge = jnp.broadcast_to(margin[line : line + 1], (8, width))[None]
             first = line * apart
             if side == 0:
                 pieces += [edge, turned[first : first + apart - 1]]
@@ -427,10 +446,8 @@
         above, below = (
             act(rows[index, side, strip].astype(F32), *stats[index]) for side in range(2)
         )
-        if strip == 0:
-            above = jnp.where(outside_rows[0], 0.0, above)
-        if strip == strips - 1:
-            below = jnp.where(outside_rows[1], 0.0, below)
+        above = jnp.where(jnp.logical_and(strip == 0, outside_rows[0]), 0.0, above)
+        below = jnp.where(jnp.logical_and(strip == strips - 1, outside_rows[1]), 0.0, below)
         values = jnp.concatenate([above[None], inner, below[None]], axis=0)
         main = values[..., :MAIN].astype(BF16)
         rest = tails(values)
@@ -457,46 +474,49 @@
         )
         return jnp.concatenate([main, ends[:, : channels - MAIN]], axis=1)
 
-    fresh = {}
-
-    def begin(index, strip):
-        span = slice(strip * SH, strip * SH + SH)
-        if index == 0:
-            inner = act(tile[span].astype(F32), *stats[0])
-        else:
-            inner = act(fresh[strip].astype(F32), *stats[1])
-        return multiply(index, strip, inner)
-
-    def finish(index, strip, products):
-        span = slice(strip * SH, strip * SH + SH)
-        live = refresh[0, strip] > 0
-        summed = collect(index, strip, products)
-        if index == 0:
-            value = (summed + shift[...].reshape(1, channels)).astype(BF16).reshape(SH, tile_cols, channels)
-            fresh[strip] = value
-            hidden[span] = jnp.where(live, value, stale_hid[span])
-            made, out = hidden, hidden_out
-        else:
-            value = tile[span].astype(F32) + summed.reshape(SH, tile_cols, channels)
-            finished[span] = jnp.where(live, value.astype(BF16), tile[span])
-            made, out = finished, block_out
-        pltpu.make_async_copy(made.at[span], out.at[span], store_sem.at[index]).start()
-
     loads[0].wait()
     margin_terms(0)
-    jobs = [(index, strip) for half in range(0, strips, AHEAD) for index in range(2) for strip in range(half, half + AHEAD)]
-    waiting, done = [], []
-    for job in jobs:
-        waiting.append((*job, begin(*job)))
-        if len(waiting) > DEPTH:
-            if len(done) == 0:
-                for copy in loads[1:]:
-                    copy.wait()
-                margin_terms(1)
-            done.append(waiting[0][:2])
-            finish(*waiting.pop(0))
-    for job in waiting:
-        finish(*job)
+    for copy in loads[1:]:
+        copy.wait()
+    margin_terms(1)
+
+    def one_pair(pair, carry):
+        places = [order[2 * pair + local] for local in range(2)]
+        spans = [pl.ds(strip * SH, SH) for strip in places]
+        lives = [refresh[0, strip] > 0 for strip in places]
+        fresh = [None, None]
+
+        def begin(index, local):
+            if index == 0:
+                inner = act(tile[spans[local]].astype(F32), *stats[0])
+            else:
+                inner = act(fresh[local].astype(F32), *stats[1])
+            return multiply(index, places[local], inner)
+
+        def finish(index, local, products):
+            span, live = spans[local], lives[local]
+            summed = collect(index, places[local], products)
+            if index == 0:
+                value = (summed + shift[...].reshape(1, channels)).astype(BF16)
+                fresh[local] = value.reshape(SH, tile_cols, channels)
+                hidden[span] = jnp.where(live, fresh[local], stale_hid[span])
+                made, out = hidden, hidden_out
+            else:
+                value = tile[span].astype(F32) + summed.reshape(SH, tile_cols, channels)
+                finished[span] = jnp.where(live, value.astype(BF16), tile[span])
+                made, out = finished, block_out
+            pltpu.make_async_copy(made.at[span], out.at[span], store_sem.at[index]).start()
+
+        waiting = None
+        for index, local in ((0, 0), (0, 1), (1, 0), (1, 1)):
+            products = begin(index, local)
+            if waiting is not None:
+                finish(*waiting)
+            waiting = (index, local, products)
+        finish(*waiting)
+        return carry
+
+    lax.fori_loop(0, pairs, one_pair, 0)
     total_wait(hidden, store_sem.at[0])
     total_wait(finished, store_sem.at[1])
 
@@ -517,6 +537,7 @@
 ):
     tile_shape = tile.shape
     tile_rows, tile_cols, channels = tile_shape
+    strip_total = tile_rows // SH
     anywhere = pl.BlockSpec(memory_space=pl.ANY)
     vmem = pl.BlockSpec(memory_space=pltpu.VMEM)
     out = jax.ShapeDtypeStruct(tile_shape, BF16)
@@ -529,6 +550,7 @@
             pltpu.VMEM((4 * MAIN, 4 * MAIN), BF16),
             pltpu.VMEM((4 * MAIN, 4 * MAIN), BF16),
             pltpu.VMEM(tile_shape, BF16),
+            pltpu.SMEM((strip_total,), jnp.int32),
             pltpu.VMEM(cols.shape, F32),
             pltpu.VMEM((2, 2, tile_rows, MAIN + LANES), F32),
             pltpu.VMEM(tile_shape, BF16),

time: 34.5 us -> 69.3 us (2.01)
  the two profiles are of different devices: /device:TPU:1 before, /device:TPU:8 now
where the time goes in v4:
time: 69.3 us; the launch traced here: 69.2 us
  Pallas kernels  68.5 us (99%)
  between operations  0.7 us (1%)
    pallas_call x1, Pallas kernels, refreshed(): pl.pallas_call(functools.partial(strips_kernel, shape), out_shape=(out, o...  49.4 us
    pallas_call x1, Pallas kernels, margins(): pl.pallas_call(functools.partial(margins_kernel, cell_count, shape), out_...  19.2 us

profile of v4, /device:TPU:8, one launch (start us, length us, event | category | flops | bytes accessed | tf_op | source)
XLA Modules:
  0.0 69.2 jit_solution(16256142766575220172)
XLA Ops:
  0.6 0.0 copy-start
  0.6 0.0 copy-start.1
  0.7 0.0 copy-start.2
  0.7 0.0 copy-start.3
  0.7 19.2 %margins.1 = (f32[8,128]{1,0:T(8,128)S(1)}, bf16[2,2,8,32,320]{4,3,2,1,0:T(8,128)(2,1)S(1)}, f32[2,2,80,320]{3,2,1,0:T(8,128)S(1)}, bf16[64,32,320]{2,1,0:T(8,12...) custom-call(bf16[64,32,320]{2,1,0:T(8,128)(2,1)} %stale_in.1, bf16[64,32,320]{2,1,0:T(8,128)(2,1)} %far_hidden.1, ...), custom_call_target="tpu_custom_call" | custom-call | tf_op jit(solution)/shard_map/margins/pallas_call | solution.py:277
  19.8 0.0 copy-done
  19.8 0.0 copy-done.1
  19.9 0.0 copy-done.2
  19.9 0.0 copy-done.3
  19.9 49.4 %strips.1 = (bf16[64,32,320]{2,1,0:T(8,128)(2,1)}, bf16[64,32,320]{2,1,0:T(8,128)(2,1)}) custom-call(s32[1,8]{1,0:T(1,128)S(1)} %bitcast.1, f32[8,128]{1,0:T(8,128)S(1)} %get-tuple-element.8.totals, f32[320]{0:T(512)S(1)} %copy-done, f32[320]{0:T(512)S(1)} %copy-done.1, bf16[2,2,8,32,320]{4,3,2,1,0:T(8,128)(2,1)S(1)} %get-tuple-element.9.rows, ...), custom_call_target="tpu_custom_call" | custom-call | tf_op jit(solution)/shard_map/strips/pallas_call | solution.py:544
Async XLA Ops:
  0.6 19.2 %copy-start = (f32[320]{0:T(512)S(1)}, f32[320]{0:T(512)}, u32[]{:S(2)}) copy-start(f32[320]{0:T(512)} %gain_one.1) | copy-start | bytes 3844
  0.6 19.2 %copy-start.1 = (f32[320]{0:T(512)S(1)}, f32[320]{0:T(512)}, u32[]{:S(2)}) copy-start(f32[320]{0:T(512)} %gain_two.1) | copy-start | bytes 3844
  0.7 19.2 %copy-start.2 = (f32[320]{0:T(512)S(1)}, f32[320]{0:T(512)}, u32[]{:S(2)}) copy-start(f32[320]{0:T(512)} %shift.1) | copy-start | bytes 3844
  0.7 19.2 %copy-start.3 = (s32[8,1]{0,1:T(1,128)S(1)}, s32[8,1]{0,1:T(1,128)}, u32[]{:S(2)}) copy-start(s32[8,1]{0,1:T(1,128)} %param.12) | copy-start | bytes 100

commit v5 on v4

--- a/solution.py
+++ b/solution.py
@@ -388,14 +388,6 @@
         flag = refresh[0, strip]
         order[jnp.where(flag > 0, before, live_total + strip - before)] = jnp.int32(strip)
         before += flag
-    for place in range(strips):
-
-        @pl.when(place >= 2 * pairs)
-        def _():
-            span = pl.ds(order[place] * SH, SH)
-            pltpu.make_async_copy(far_hidden.at[span], hidden_out.at[span], store_sem.at[0]).start()
-            pltpu.make_async_copy(tile.at[span], block_out.at[span], store_sem.at[1]).start()
-
     n_row, n_col = shape
     row, col = lax.axis_index("row"), lax.axis_index("col")
     outside_rows = (row == 0, row == n_row - 1)
@@ -517,6 +509,14 @@
         return carry
 
     lax.fori_loop(0, pairs, one_pair, 0)
+    for place in range(strips):
+
+        @pl.when(place >= 2 * pairs)
+        def _():
+            span = pl.ds(order[place] * SH, SH)
+            pltpu.make_async_copy(stale_hid.at[span], hidden_out.at[span], store_sem.at[0]).start()
+            pltpu.make_async_copy(tile.at[span], block_out.at[span], store_sem.at[1]).start()
+
     total_wait(hidden, store_sem.at[0])
     total_wait(finished, store_sem.at[1])
 

time: 69.3 us -> 34 us (0.49)
  the two profiles are of different devices: /device:TPU:8 before, /device:TPU:1 now
where the time goes in v5:
time: 34 us; the launch traced here: 33.4 us
  Pallas kernels  32.6 us (96%)
  between operations  0.7 us (2%)
    pallas_call x1, Pallas kernels, margins(): pl.pallas_call(functools.partial(margins_kernel, cell_count, shape), out_...  20.3 us
    pallas_call x1, Pallas kernels, refreshed(): pl.pallas_call(functools.partial(strips_kernel, shape), out_shape=(out, o...  12.4 us

profile of v5, /device:TPU:1, one launch (start us, length us, event | category | flops | bytes accessed | tf_op | source)
XLA Modules:
  0.0 33.4 jit_solution(5900002587747593170)
XLA Ops:
  0.6 0.0 copy-start
  0.6 0.0 copy-start.1
  0.7 0.0 copy-start.2
  0.7 0.0 copy-start.3
  0.7 20.3 %margins.1 = (f32[8,128]{1,0:T(8,128)S(1)}, bf16[2,2,8,32,320]{4,3,2,1,0:T(8,128)(2,1)S(1)}, f32[2,2,80,320]{3,2,1,0:T(8,128)S(1)}, bf16[64,32,320]{2,1,0:T(8,12...) custom-call(bf16[64,32,320]{2,1,0:T(8,128)(2,1)} %stale_in.1, bf16[64,32,320]{2,1,0:T(8,128)(2,1)} %far_hidden.1, ...), custom_call_target="tpu_custom_call" | custom-call | tf_op jit(solution)/shard_map/margins/pallas_call | solution.py:277
  21.0 0.0 copy-done
  21.0 0.0 copy-done.1
  21.0 0.0 copy-done.2
  21.0 0.0 copy-done.3
  21.0 12.4 %strips.1 = (bf16[64,32,320]{2,1,0:T(8,128)(2,1)}, bf16[64,32,320]{2,1,0:T(8,128)(2,1)}) custom-call(s32[1,8]{1,0:T(1,128)S(1)} %bitcast.1, f32[8,128]{1,0:T(8,128)S(1)} %get-tuple-element.8.totals, f32[320]{0:T(512)S(1)} %copy-done, f32[320]{0:T(512)S(1)} %copy-done.1, bf16[2,2,8,32,320]{4,3,2,1,0:T(8,128)(2,1)S(1)} %get-tuple-element.9.rows, ...), custom_call_target="tpu_custom_call" | custom-call | tf_op jit(solution)/shard_map/strips/pallas_call | solution.py:544
Async XLA Ops:
  0.6 20.3 %copy-start = (f32[320]{0:T(512)S(1)}, f32[320]{0:T(512)}, u32[]{:S(2)}) copy-start(f32[320]{0:T(512)} %gain_one.1) | copy-start | bytes 3844
  0.6 20.3 %copy-start.1 = (f32[320]{0:T(512)S(1)}, f32[320]{0:T(512)}, u32[]{:S(2)}) copy-start(f32[320]{0:T(512)} %gain_two.1) | copy-start | bytes 3844
  0.7 20.3 %copy-start.2 = (f32[320]{0:T(512)S(1)}, f32[320]{0:T(512)}, u32[]{:S(2)}) copy-start(f32[320]{0:T(512)} %shift.1) | copy-start | bytes 3844
  0.7 20.3 %copy-start.3 = (s32[8,1]{0,1:T(1,128)S(1)}, s32[8,1]{0,1:T(1,128)}, u32[]{:S(2)}) copy-start(s32[8,1]{0,1:T(1,128)} %param.12) | copy-start | bytes 100

commit v6 on v5

--- a/solution.py
+++ b/solution.py
@@ -382,7 +382,7 @@
         copy.start()
     weights = (first_weights, second_weights)
     live_total = sum(refresh[0, strip] for strip in range(strips))
-    pairs = lax.div(live_total + 1, 2)
+    pairs = jnp.maximum(lax.div(live_total + 1, 2), 1)
     before = jnp.int32(0)
     for strip in range(strips):
         flag = refresh[0, strip]
@@ -434,7 +434,7 @@
         at = 0 if side == 0 else 7
         return jnp.where(sub == at, carried, turned).reshape(cells, width)
 
-    def multiply(index, strip, inner):
+    def windows(index, strip, inner):
         above, below = (
             act(rows[index, side, strip].astype(F32), *stats[index]) for side in range(2)
         )
@@ -443,9 +443,11 @@
         values = jnp.concatenate([above[None], inner, below[None]], axis=0)
         main = values[..., :MAIN].astype(BF16)
         rest = tails(values)
-        wide = side_by_side(
+        return side_by_side(
             [main[a : a + SH] for a in range(3)], [rest[a : a + SH] for a in range(3)]
         ).reshape(cells, 4 * MAIN)
+
+    def multiply(index, wide):
         return [
             jnp.dot(
                 wide,
@@ -466,24 +468,18 @@
         )
         return jnp.concatenate([main, ends[:, : channels - MAIN]], axis=1)
 
-    loads[0].wait()
-    margin_terms(0)
-    for copy in loads[1:]:
-        copy.wait()
-    margin_terms(1)
-
-    def one_pair(pair, carry):
+    def one_pair(pair, carry, opening=False):
         places = [order[2 * pair + local] for local in range(2)]
         spans = [pl.ds(strip * SH, SH) for strip in places]
         lives = [refresh[0, strip] > 0 for strip in places]
         fresh = [None, None]
 
-        def begin(index, local):
+        def enter(index, local):
             if index == 0:
                 inner = act(tile[spans[local]].astype(F32), *stats[0])
             else:
                 inner = act(fresh[local].astype(F32), *stats[1])
-            return multiply(index, places[local], inner)
+            return windows(index, places[local], inner)
 
         def finish(index, local, products):
             span, live = spans[local], lives[local]
@@ -499,16 +495,25 @@
                 made, out = finished, block_out
             pltpu.make_async_copy(made.at[span], out.at[span], store_sem.at[index]).start()
 
-        waiting = None
-        for index, local in ((0, 0), (0, 1), (1, 0), (1, 1)):
-            products = begin(index, local)
-            if waiting is not None:
-                finish(*waiting)
-            waiting = (index, local, products)
-        finish(*waiting)
+        wides = [enter(0, local) for local in range(2)]
+        if opening:
+            loads[0].wait()
+        waiting = multiply(0, wides[0])
+        products = multiply(0, wides[1])
+        if opening:
+            margin_terms(0)
+            for copy in loads[1:]:
+                copy.wait()
+            margin_terms(1)
+        finish(0, 0, waiting)
+        waiting, products = products, multiply(1, enter(1, 0))
+        finish(0, 1, waiting)
+        waiting, products = products, multiply(1, enter(1, 1))
+        finish(1, 0, waiting)
+        finish(1, 1, products)
         return carry
 
-    lax.fori_loop(0, pairs, one_pair, 0)
+    one_pair(0, 0, opening=True)
     for place in range(strips):
 
         @pl.when(place >= 2 * pairs)
@@ -517,6 +522,7 @@
             pltpu.make_async_copy(stale_hid.at[span], hidden_out.at[span], store_sem.at[0]).start()
             pltpu.make_async_copy(tile.at[span], block_out.at[span], store_sem.at[1]).start()
 
+    lax.fori_loop(1, pairs, one_pair, 0)
     total_wait(hidden, store_sem.at[0])
     total_wait(finished, store_sem.at[1])
 

time: 34 us -> 34.6 us (1.018)
  the two profiles are of different devices: /device:TPU:1 before, /device:TPU:32 now
where the time goes in v6:
time: 34.6 us; the launch traced here: 34.5 us
  Pallas kernels  33.8 us (98%)
  between operations  0.7 us (2%)
    pallas_call x1, Pallas kernels, margins(): pl.pallas_call(functools.partial(margins_kernel, cell_count, shape), out_...  19.3 us
    pallas_call x1, Pallas kernels, refreshed(): pl.pallas_call(functools.partial(strips_kernel, shape), out_shape=(out, o...  14.5 us

profile of v6, /device:TPU:32, one launch (start us, length us, event | category | flops | bytes accessed | tf_op | source)
XLA Modules:
  0.0 34.5 jit_solution(13445075841784475780)
XLA Ops:
  0.6 0.0 copy-start
  0.6 0.0 copy-start.1
  0.7 0.0 copy-start.2
  0.7 0.0 copy-start.3
  0.7 19.3 %margins.1 = (f32[8,128]{1,0:T(8,128)S(1)}, bf16[2,2,8,32,320]{4,3,2,1,0:T(8,128)(2,1)S(1)}, f32[2,2,80,320]{3,2,1,0:T(8,128)S(1)}, bf16[64,32,320]{2,1,0:T(8,12...) custom-call(bf16[64,32,320]{2,1,0:T(8,128)(2,1)} %stale_in.1, bf16[64,32,320]{2,1,0:T(8,128)(2,1)} %far_hidden.1, ...), custom_call_target="tpu_custom_call" | custom-call | tf_op jit(solution)/shard_map/margins/pallas_call | solution.py:277
  20.0 0.0 copy-done
  20.0 0.0 copy-done.1
  20.0 0.0 copy-done.2
  20.0 0.0 copy-done.3
  20.0 14.5 %strips.1 = (bf16[64,32,320]{2,1,0:T(8,128)(2,1)}, bf16[64,32,320]{2,1,0:T(8,128)(2,1)}) custom-call(s32[1,8]{1,0:T(1,128)S(1)} %bitcast.1, f32[8,128]{1,0:T(8,128)S(1)} %get-tuple-element.8.totals, f32[320]{0:T(512)S(1)} %copy-done, f32[320]{0:T(512)S(1)} %copy-done.1, bf16[2,2,8,32,320]{4,3,2,1,0:T(8,128)(2,1)S(1)} %get-tuple-element.9.rows, ...), custom_call_target="tpu_custom_call" | custom-call | tf_op jit(solution)/shard_map/strips/pallas_call | solution.py:550
Async XLA Ops:
  0.6 19.4 %copy-start = (f32[320]{0:T(512)S(1)}, f32[320]{0:T(512)}, u32[]{:S(2)}) copy-start(f32[320]{0:T(512)} %gain_one.1) | copy-start | bytes 3844
  0.6 19.4 %copy-start.1 = (f32[320]{0:T(512)S(1)}, f32[320]{0:T(512)}, u32[]{:S(2)}) copy-start(f32[320]{0:T(512)} %gain_two.1) | copy-start | bytes 3844
  0.7 19.4 %copy-start.2 = (f32[320]{0:T(512)S(1)}, f32[320]{0:T(512)}, u32[]{:S(2)}) copy-start(f32[320]{0:T(512)} %shift.1) | copy-start | bytes 3844
  0.7 19.4 %copy-start.3 = (s32[8,1]{0,1:T(1,128)S(1)}, s32[8,1]{0,1:T(1,128)}, u32[]{:S(2)}) copy-start(s32[8,1]{0,1:T(1,128)} %param.12) | copy-start | bytes 100

commit v7 on v6

--- a/solution.py
+++ b/solution.py
@@ -15,6 +15,7 @@
 F32 = jnp.float32
 BF16 = jnp.bfloat16
 MAIN = 256
+AHEAD = 4
 
 
 def act(values, center, half_scale):
@@ -468,26 +469,26 @@
         )
         return jnp.concatenate([main, ends[:, : channels - MAIN]], axis=1)
 
-    def one_pair(pair, carry, opening=False):
-        places = [order[2 * pair + local] for local in range(2)]
-        spans = [pl.ds(strip * SH, SH) for strip in places]
-        lives = [refresh[0, strip] > 0 for strip in places]
-        fresh = [None, None]
-
-        def enter(index, local):
+    def straight(places, others):
+        fresh = {}
+
+        def span_of(place):
+            return pl.ds(places[place] * SH, SH)
+
+        def begin(index, place):
             if index == 0:
-                inner = act(tile[spans[local]].astype(F32), *stats[0])
+                inner = act(tile[span_of(place)].astype(F32), *stats[0])
             else:
-                inner = act(fresh[local].astype(F32), *stats[1])
-            return windows(index, places[local], inner)
-
-        def finish(index, local, products):
-            span, live = spans[local], lives[local]
-            summed = collect(index, places[local], products)
+                inner = act(fresh[place].astype(F32), *stats[1])
+            return multiply(index, windows(index, places[place], inner))
+
+        def finish(index, place, products):
+            span, live = span_of(place), refresh[0, places[place]] > 0
+            summed = collect(index, places[place], products)
             if index == 0:
                 value = (summed + shift[...].reshape(1, channels)).astype(BF16)
-                fresh[local] = value.reshape(SH, tile_cols, channels)
-                hidden[span] = jnp.where(live, fresh[local], stale_hid[span])
+                fresh[place] = value.reshape(SH, tile_cols, channels)
+                hidden[span] = jnp.where(live, fresh[place], stale_hid[span])
                 made, out = hidden, hidden_out
             else:
                 value = tile[span].astype(F32) + summed.reshape(SH, tile_cols, channels)
@@ -495,34 +496,41 @@
                 made, out = finished, block_out
             pltpu.make_async_copy(made.at[span], out.at[span], store_sem.at[index]).start()
 
-        wides = [enter(0, local) for local in range(2)]
-        if opening:
-            loads[0].wait()
-        waiting = multiply(0, wides[0])
-        products = multiply(0, wides[1])
-        if opening:
-            margin_terms(0)
-            for copy in loads[1:]:
-                copy.wait()
-            margin_terms(1)
-        finish(0, 0, waiting)
-        waiting, products = products, multiply(1, enter(1, 0))
-        finish(0, 1, waiting)
-        waiting, products = products, multiply(1, enter(1, 1))
-        finish(1, 0, waiting)
-        finish(1, 1, products)
-        return carry
-
-    one_pair(0, 0, opening=True)
-    for place in range(strips):
-
-        @pl.when(place >= 2 * pairs)
+        loads[0].wait()
+        margin_terms(0)
+        waiting, waited = [], False
+        for start in range(0, len(places), AHEAD):
+            for index in range(2):
+                for place in range(start, min(start + AHEAD, len(places))):
+                    waiting.append((index, place, begin(index, place)))
+                    if len(waiting) < 2:
+                        continue
+                    if not waited:
+                        for copy in loads[1:]:
+                            copy.wait()
+                        margin_terms(1)
+                        for strip in others:
+                            span = pl.ds(strip * SH, SH)
+                            pltpu.make_async_copy(
+                                stale_hid.at[span], hidden_out.at[span], store_sem.at[0]
+                            ).start()
+                            pltpu.make_async_copy(
+                                tile.at[span], block_out.at[span], store_sem.at[1]
+                            ).start()
+                        waited = True
+                    finish(*waiting.pop(0))
+        finish(*waiting.pop(0))
+
+    for count in range(1, strips // 2 + 1):
+
+        @pl.when(pairs == count)
         def _():
-            span = pl.ds(order[place] * SH, SH)
-            pltpu.make_async_copy(stale_hid.at[span], hidden_out.at[span], store_sem.at[0]).start()
-            pltpu.make_async_copy(tile.at[span], block_out.at[span], store_sem.at[1]).start()
-
-    lax.fori_loop(1, pairs, one_pair, 0)
+            if 2 * count == strips:
+                listed = list(range(strips))
+            else:
+                listed = [order[place] for place in range(strips)]
+            straight(listed[: 2 * count], listed[2 * count :])
+
     total_wait(hidden, store_sem.at[0])
     total_wait(finished, store_sem.at[1])
 

time: 34.6 us -> 34.3 us (level); the launches traced: 34.5 us -> 33.7 us
  Pallas kernels: 33.8 us -> 32.8 us
    pallas_call x1, Pallas kernels: 14.5 us -> 13.5 us  [refreshed(): pl.pallas_call(functools.partial(strips_kernel, shape), out_shape=(out, o...]
where the time goes in v7:
time: 34.3 us; the launch traced here: 33.7 us
  Pallas kernels  32.8 us (96%)
  between operations  0.88 us (3%)
    pallas_call x1, Pallas kernels, margins(): pl.pallas_call(functools.partial(margins_kernel, cell_count, shape), out_...  19.3 us
    pallas_call x1, Pallas kernels, refreshed(): pl.pallas_call(functools.partial(strips_kernel, shape), out_shape=(out, o...  13.5 us

profile of v7, /device:TPU:32, one launch (start us, length us, event | category | flops | bytes accessed | tf_op | source)
XLA Modules:
  0.0 33.7 jit_solution(13719236139801285612)
XLA Ops:
  0.6 0.0 copy-start
  0.6 0.0 copy-start.1
  0.7 0.0 copy-start.2
  0.7 0.0 copy-start.3
  0.7 19.3 %margins.1 = (f32[8,128]{1,0:T(8,128)S(1)}, bf16[2,2,8,32,320]{4,3,2,1,0:T(8,128)(2,1)S(1)}, f32[2,2,80,320]{3,2,1,0:T(8,128)S(1)}, bf16[64,32,320]{2,1,0:T(8,12...) custom-call(bf16[64,32,320]{2,1,0:T(8,128)(2,1)} %stale_in.1, bf16[64,32,320]{2,1,0:T(8,128)(2,1)} %far_hidden.1, ...), custom_call_target="tpu_custom_call" | custom-call | tf_op jit(solution)/shard_map/margins/pallas_call | solution.py:278
  20.0 0.0 copy-done
  20.0 0.0 copy-done.1
  20.0 0.0 copy-done.2
  20.0 0.0 copy-done.3
  20.0 13.5 %strips.1 = (bf16[64,32,320]{2,1,0:T(8,128)(2,1)}, bf16[64,32,320]{2,1,0:T(8,128)(2,1)}) custom-call(s32[1,8]{1,0:T(1,128)S(1)} %bitcast.1, f32[8,128]{1,0:T(8,128)S(1)} %get-tuple-element.8.totals, f32[320]{0:T(512)S(1)} %copy-done, f32[320]{0:T(512)S(1)} %copy-done.1, bf16[2,2,8,32,320]{4,3,2,1,0:T(8,128)(2,1)S(1)} %get-tuple-element.9.rows, ...), custom_call_target="tpu_custom_call" | custom-call | tf_op jit(solution)/shard_map/strips/pallas_call | solution.py:558
Async XLA Ops:
  0.6 19.4 %copy-start = (f32[320]{0:T(512)S(1)}, f32[320]{0:T(512)}, u32[]{:S(2)}) copy-start(f32[320]{0:T(512)} %gain_one.1) | copy-start | bytes 3844
  0.6 19.4 %copy-start.1 = (f32[320]{0:T(512)S(1)}, f32[320]{0:T(512)}, u32[]{:S(2)}) copy-start(f32[320]{0:T(512)} %gain_two.1) | copy-start | bytes 3844
  0.7 19.4 %copy-start.2 = (f32[320]{0:T(512)S(1)}, f32[320]{0:T(512)}, u32[]{:S(2)}) copy-start(f32[320]{0:T(512)} %shift.1) | copy-start | bytes 3844
  0.7 19.4 %copy-start.3 = (s32[8,1]{0,1:T(1,128)S(1)}, s32[8,1]{0,1:T(1,128)}, u32[]{:S(2)}) copy-start(s32[8,1]{0,1:T(1,128)} %param.12) | copy-start | bytes 100

commit v8 on v7

--- a/solution.py
+++ b/solution.py
@@ -102,6 +102,19 @@
             barrier, inc=1, device_id=device, device_id_type=pl.DeviceIdType.MESH
         )
 
+    barrier = pltpu.get_barrier_semaphore()
+
+    @pl.loop(0, first_peers)
+    def _(step):
+        signal(first_peer(step))
+        signal(second_peer(step))
+
+    for place in (up, row, down):
+        for device in ((place, left), (place, right)):
+            signal(device)
+    signal((up, col))
+    signal((down, col))
+
     loads = []
     half = tile_rows // 2
     for index, source in enumerate((stale_in, stale_hid)):
@@ -120,19 +133,6 @@
     ]
     for copy in late:
         copy.start()
-
-    barrier = pltpu.get_barrier_semaphore()
-
-    @pl.loop(0, first_peers)
-    def _(step):
-        signal(first_peer(step))
-        signal(second_peer(step))
-
-    for place in (up, row, down):
-        for device in ((place, left), (place, right)):
-            signal(device)
-    signal((up, col))
-    signal((down, col))
 
     lines = lax.broadcasted_iota(jnp.int32, (channels, LANES), 0)
     lanes = lax.rem(lax.broadcasted_iota(jnp.int32, (channels, LANES), 1), GROUPS)

time: 34.3 us -> 33.9 us (0.988)
  the two profiles are of different devices: /device:TPU:32 before, /device:TPU:34 now
where the time goes in v8:
time: 33.9 us; the launch traced here: 33.8 us
  Pallas kernels  32.9 us (97%)
  between operations  0.88 us (3%)
    pallas_call x1, Pallas kernels, margins(): pl.pallas_call(functools.partial(margins_kernel, cell_count, shape), out_...  19.3 us
    pallas_call x1, Pallas kernels, refreshed(): pl.pallas_call(functools.partial(strips_kernel, shape), out_shape=(out, o...  13.5 us

profile of v8, /device:TPU:34, one launch (start us, length us, event | category | flops | bytes accessed | tf_op | source)
XLA Modules:
  0.0 33.8 jit_solution(8124556324837242599)
XLA Ops:
  0.6 0.0 copy-start
  0.6 0.0 copy-start.1
  0.7 0.0 copy-start.2
  0.7 0.0 copy-start.3
  0.7 19.3 %margins.1 = (f32[8,128]{1,0:T(8,128)S(1)}, bf16[2,2,8,32,320]{4,3,2,1,0:T(8,128)(2,1)S(1)}, f32[2,2,80,320]{3,2,1,0:T(8,128)S(1)}, bf16[64,32,320]{2,1,0:T(8,12...) custom-call(bf16[64,32,320]{2,1,0:T(8,128)(2,1)} %stale_in.1, bf16[64,32,320]{2,1,0:T(8,128)(2,1)} %far_hidden.1, ...), custom_call_target="tpu_custom_call" | custom-call | tf_op jit(solution)/shard_map/margins/pallas_call | solution.py:278
  20.0 0.0 copy-done
  20.0 0.0 copy-done.1
  20.0 0.0 copy-done.2
  20.0 0.0 copy-done.3
  20.0 13.5 %strips.1 = (bf16[64,32,320]{2,1,0:T(8,128)(2,1)}, bf16[64,32,320]{2,1,0:T(8,128)(2,1)}) custom-call(s32[1,8]{1,0:T(1,128)S(1)} %bitcast.1, f32[8,128]{1,0:T(8,128)S(1)} %get-tuple-element.8.totals, f32[320]{0:T(512)S(1)} %copy-done, f32[320]{0:T(512)S(1)} %copy-done.1, bf16[2,2,8,32,320]{4,3,2,1,0:T(8,128)(2,1)S(1)} %get-tuple-element.9.rows, ...), custom_call_target="tpu_custom_call" | custom-call | tf_op jit(solution)/shard_map/strips/pallas_call | solution.py:558
Async XLA Ops:
  0.6 19.4 %copy-start = (f32[320]{0:T(512)S(1)}, f32[320]{0:T(512)}, u32[]{:S(2)}) copy-start(f32[320]{0:T(512)} %gain_one.1) | copy-start | bytes 3844
  0.6 19.4 %copy-start.1 = (f32[320]{0:T(512)S(1)}, f32[320]{0:T(512)}, u32[]{:S(2)}) copy-start(f32[320]{0:T(512)} %gain_two.1) | copy-start | bytes 3844
  0.7 19.4 %copy-start.2 = (f32[320]{0:T(512)S(1)}, f32[320]{0:T(512)}, u32[]{:S(2)}) copy-start(f32[320]{0:T(512)} %shift.1) | copy-start | bytes 3844
  0.7 19.4 %copy-start.3 = (s32[8,1]{0,1:T(1,128)S(1)}, s32[8,1]{0,1:T(1,128)}, u32[]{:S(2)}) copy-start(s32[8,1]{0,1:T(1,128)} %param.12) | copy-start | bytes 100
